TPU v7x, 128 devices: a whole 4x4x4 slice. The times are simulated.
128 devices in a mesh: dp: 16 (over y, x), ctx: 4 (over z), tensor: 2 (over core).
Axes of the slice: x: 4, y: 4, z: 4, core: 2. Of those that a mesh axis runs over, the one named last changes fastest.
Arguments:
- tokens: bfloat16 [16, 2048, 640], P('dp', 'ctx'), may hold values from -6 to 6
- segments: int32 [16, 2048], P('dp', 'ctx'), may hold values from 0 to 8, as said below
- cotangent: bfloat16 [16, 2048, 640], P('dp', 'ctx'), may hold values from -6 to 6
- w_query: bfloat16 [640, 1024], P('dp', 'tensor'), may hold values from -0.25 to 0.25
- w_keyval: bfloat16 [640, 512], P('dp'), may hold values from -0.25 to 0.25
- w_out: bfloat16 [1024, 640], P('tensor', 'dp'), may hold values from -0.1875 to 0.1875
- w_gateup: bfloat16 [2, 640, 2048], P(None, 'dp', 'tensor'), may hold values from -0.25 to 0.25
- w_down: bfloat16 [2048, 640], P('tensor', 'dp'), may hold values from -0.125 to 0.125
- norm_gains: bfloat16 [4, 640], P(None, 'dp'), may hold values from 0.099609375 to 1.8984375
- head_gains: bfloat16 [2, 256], P(None, 'dp'), may hold values from 0.099609375 to 1.8984375
Outputs:
- output: bfloat16 [16, 2048, 640], P('dp', 'ctx')
- input_grad: float32 [16, 2048, 640], P('dp', 'ctx')
- grad_query: float32 [640, 1024], P('dp', 'tensor')
- grad_keyval: float32 [640, 512], P('dp')
- grad_out: float32 [1024, 640], P('tensor', 'dp')
- grad_gateup: float32 [2, 640, 2048], P(None, 'dp', 'tensor')
- grad_down: float32 [2048, 640], P('tensor', 'dp')
- grad_norm_gains: float32 [4, 640], P(None, 'dp')
- grad_head_gains: float32 [2, 256], P(None, 'dp')
Inputs may be any that keep to these rules, and one draw needn't show every extreme that they name: `segments`: segment numbers never fall along a sequence. In every sequence exactly 4 boundaries fall among its first 512 positions and 4 among its last 512, so one document runs from the first of those ranges to the last.
All inputs are finite; a program needn't handle non-finite values.
Results may differ from a plain program's by a relative error of at most 0.025.
Values may be sent and summed in bfloat16 or wider, within the bound.
A program may use at most 128 MiB of HBM per device.

v0:
```python
import math
import types

import jax
import jax.numpy as jnp
from jax import lax
from jax.experimental import pallas as pl
from jax.experimental.pallas import tpu as pltpu
from jax.sharding import PartitionSpec as P

WINDOW = 512
EPSILON = 1e-06
MESH = pl.DeviceIdType.MESH
VMEM_BYTES = 60 * 1024 * 1024

KV, QUERY, EXTRA, OUT, GATEUP, DOWN, WIRE = 0, 128, 384, 512, 768, 1792, 2304
GATHERS = (
    ((0, 256), (256, 256)),
    ((512, 128), (640, 128)),
    ((768, 512), (1280, 512)),
    ((1792, 256), (2048, 256)),
)
SCATTERS = (
    ((0, 256), (256, 128)),
    ((512, 128), (640, 128)),
    ((768, 512), (1280, 512)),
    ((1792, 256), (2048, 256)),
    (None, (384, 128)),
)
SET_COLS = 1152
CUT = 48
ROWS, D, HD, FFH = 512, 640, 256, 1024
SCALE = 1.0 / math.sqrt(HD)
LOW = jnp.bfloat16
F32 = jnp.float32
NN, NT, TN = ((1,), (0,)), ((1,), (1,)), ((0,), (0,))


def place(u):
    return lax.rem(u + 8, 4)


class Wires:
    def __init__(self, send, recv):
        self.send, self.recv, self.used = send, recv, 0
        self.started = []

    def copy(self, src, dst, target):
        index = self.used
        self.used += 1
        made = pltpu.make_async_remote_copy(
            src_ref=src,
            dst_ref=dst,
            send_sem=self.send.at[index],
            recv_sem=self.recv.at[index],
            device_id=target,
            device_id_type=MESH,
        )
        made.start()
        self.started.append(made)
        return made

    def drain(self):
        for made in self.started:
            made.wait_send()
        self.started = []


class Ring:
    def __init__(self, first, x, y):
        self.first = first
        self.f, self.s = (x, y) if first == "x" else (y, x)

    def slot(self, ref, f, s, *rest):
        return ref.at[(s, f) + rest] if self.first == "x" else ref.at[(f, s) + rest]

    def index(self, f, s):
        return (s, f) if self.first == "x" else (f, s)

    def to_f(self, step):
        f = place(self.f + step)
        return {"dp": self.s * 4 + f} if self.first == "x" else {"dp": f * 4 + self.s}

    def to_s(self, step):
        s = place(self.s + step)
        return {"dp": s * 4 + self.f} if self.first == "x" else {"dp": self.f * 4 + s}


class Gather:
    def __init__(self, ring, wires, shard, whole, start, width):
        self.ring, self.wires, self.shard, self.whole = ring, wires, shard, whole
        self.cols = pl.ds(start, width)

    def one(self):
        r, c = self.ring, self.cols
        src = self.shard.at[:, c]
        dst = r.slot(self.whole, r.f, r.s, slice(None), c)
        self.a = self.wires.copy(src, dst, r.to_f(1))
        self.b = self.wires.copy(src, dst, r.to_f(-1))

    def two(self):
        r, c = self.ring, self.cols
        self.a.wait_recv()
        part = r.slot(self.whole, place(r.f - 1), r.s, pl.ds(0, CUT), c)
        a = self.wires.copy(part, part, r.to_f(1))
        self.b.wait_recv()
        part = r.slot(self.whole, place(r.f + 1), r.s, pl.ds(CUT, 80 - CUT), c)
        b = self.wires.copy(part, part, r.to_f(-1))
        self.a, self.b = a, b

    def three(self):
        r, c = self.ring, self.cols
        self.a.wait_recv()
        self.b.wait_recv()
        part = r.slot(self.whole, slice(None), r.s, slice(None), c)
        self.a = self.wires.copy(part, part, r.to_s(1))
        self.b = self.wires.copy(part, part, r.to_s(-1))

    def four(self):
        r, c = self.ring, self.cols
        self.a.wait_recv()
        part = r.slot(self.whole, pl.ds(0, 2), place(r.s - 1), slice(None), c)
        a = self.wires.copy(part, part, r.to_s(1))
        self.b.wait_recv()
        part = r.slot(self.whole, pl.ds(2, 2), place(r.s + 1), slice(None), c)
        b = self.wires.copy(part, part, r.to_s(-1))
        self.a, self.b = a, b

    def finish(self):
        self.a.wait_recv()
        self.b.wait_recv()


def added(*terms):
    total = terms[0].astype(jnp.float32)
    for term in terms[1:]:
        total = total + term.astype(jnp.float32)
    return total


class Scatter:
    def __init__(self, ring, wires, grads, bufs, final, z, start, width, offset):
        self.ring, self.wires, self.grads, self.final, self.z = ring, wires, grads, final, z
        self.r1, self.r2, self.sums, self.r3, self.r4 = bufs
        self.cols = pl.ds(start, width)
        self.near = pl.ds(offset, width)

    def one(self):
        r, c, n = self.ring, self.cols, self.near
        far = place(r.s + 2)
        self.a = self.wires.copy(
            r.slot(self.grads, pl.ds(0, 2), far, slice(None), c), self.r1.at[0, :, :, n], r.to_s(1)
        )
        self.b = self.wires.copy(
            r.slot(self.grads, pl.ds(2, 2), far, slice(None), c), self.r1.at[1, :, :, n], r.to_s(-1)
        )

    def two(self):
        r, c, n = self.ring, self.cols, self.near
        after, before = place(r.s + 1), place(r.s - 1)
        self.a.wait_recv()
        for i in range(2):
            at = r.index(i, after) + (slice(None), c)
            self.grads[at] = added(self.grads[at], self.r1[0, i, :, n]).astype(jnp.bfloat16)
        a = self.wires.copy(
            r.slot(self.grads, slice(None), after, slice(None), c), self.r2.at[0, :, :, n], r.to_s(1)
        )
        self.b.wait_recv()
        for i in range(2):
            at = r.index(2 + i, before) + (slice(None), c)
            self.grads[at] = added(self.grads[at], self.r1[1, i, :, n]).astype(jnp.bfloat16)
        b = self.wires.copy(
            r.slot(self.grads, slice(None), before, slice(None), c),
            self.r2.at[1, :, :, n],
            r.to_s(-1),
        )
        self.a, self.b = a, b

    def three(self):
        r, c, n = self.ring, self.cols, self.near
        self.a.wait_recv()
        self.b.wait_recv()
        for i in range(4):
            at = r.index(i, r.s) + (slice(None), c)
            self.sums[i, :, n] = added(
                self.grads[at], self.r2[0, i, :, n], self.r2[1, i, :, n]
            ).astype(jnp.bfloat16)
        far = place(r.f + 2)
        self.a = self.wires.copy(
            self.sums.at[far, pl.ds(0, CUT), n], self.r3.at[pl.ds(0, CUT), n], r.to_f(1)
        )
        self.b = self.wires.copy(
            self.sums.at[far, pl.ds(CUT, 80 - CUT), n],
            self.r3.at[pl.ds(CUT, 80 - CUT), n],
            r.to_f(-1),
        )

    def four(self):
        r, n = self.ring, self.near
        after, before = place(r.f + 1), place(r.f - 1)
        top, low = pl.ds(0, CUT), pl.ds(CUT, 80 - CUT)
        self.a.wait_recv()
        self.sums[after, top, n] = added(self.sums[after, top, n], self.r3[top, n]).astype(
            jnp.bfloat16
        )
        a = self.wires.copy(self.sums.at[after, :, n], self.r4.at[0, :, n], r.to_f(1))
        self.b.wait_recv()
        self.sums[before, low, n] = added(self.sums[before, low, n], self.r3[low, n]).astype(
            jnp.bfloat16
        )
        b = self.wires.copy(self.sums.at[before, :, n], self.r4.at[1, :, n], r.to_f(-1))
        self.a, self.b = a, b

    def five(self):
        r, c, n = self.ring, self.cols, self.near
        self.a.wait_recv()
        self.b.wait_recv()
        self.final[self.z, :, c] = added(
            self.sums[r.f, :, n], self.r4[0, :, n], self.r4[1, :, n]
        ).astype(jnp.bfloat16)
        part = self.final.at[self.z, :, c]
        self.zs = [self.wires.copy(part, part, {"ctx": place(self.z + k)}) for k in (1, 3, 2)]

    def finish(self):
        for made in self.zs:
            made.wait_recv()


def greet(targets):
    barrier = pltpu.get_barrier_semaphore()
    for target in targets:
        pl.semaphore_signal(barrier, inc=1, device_id=target, device_id_type=MESH)
    pl.semaphore_wait(barrier, len(targets))


def spot():
    d = lax.axis_index("dp")
    return lax.rem(d, 4), lax.div(d, 4), lax.axis_index("ctx")


def dot(a, b, dims=NN):
    return lax.dot_general(a, b, (dims, ((), ())), preferred_element_type=F32)


def rms(field):
    return lax.rsqrt(jnp.mean(field * field, axis=-1, keepdims=True) + EPSILON)


def norm_back(field, gain, grad):
    r = rms(field)
    hat = field * r
    scaled = grad * gain
    back = r * (scaled - hat * jnp.mean(scaled * hat, axis=-1, keepdims=True))
    return back, jnp.sum(grad * hat, axis=0, keepdims=True)


def turn(field, cos, sin):
    a, b = field[:, :128], field[:, 128:]
    return jnp.concatenate([a * cos - b * sin, b * cos + a * sin], axis=1)


def turn_back(field, cos, sin):
    a, b = field[:, :128], field[:, 128:]
    return jnp.concatenate([a * cos + b * sin, b * cos - a * sin], axis=1)


def fold(block):
    half = block.shape[-1] // 2
    return jnp.concatenate([block[..., :half], block[..., half:]], axis=-2)


def unfold(block):
    rows = block.shape[-2] // 2
    return jnp.concatenate([block[..., :rows, :], block[..., rows:, :]], axis=-1)


def iota(shape, axis):
    return lax.broadcasted_iota(jnp.int32, shape, axis)


SCRATCH = dict(
    wire=((80, WIRE), LOW),
    whole=((4, 4, 80, WIRE), LOW),
    pad=((1024, 128), F32),
    tall=((128, D), F32),
    wq=((D, 512), LOW),
    wkv=((D, HD), LOW),
    wo=((D, 512), LOW),
    wg=((D, FFH), LOW),
    wu=((D, FFH), LOW),
    wd=((D, FFH), LOW),
    gains=((8, D), F32),
    heads=((8, HD), F32),
    dgains=((8, D), F32),
    dheads=((8, HD), F32),
    tokh=((ROWS, D), LOW),
    segp=((1, ROWS), jnp.int32),
    lo_col=((ROWS, 128), F32),
    lo_row=((8, ROWS), F32),
    cos=((1024, 128), F32),
    sin=((1024, 128), F32),
    n1=((1024, D), LOW),
    n1t=((D, ROWS), LOW),
    kvb=((2, 1024, HD), LOW),
    kvraw=((ROWS, HD), F32),
    qraw=((4, 256, HD), F32),
    q=((4, 256, HD), LOW),
    o=((ROWS, 512), LOW),
    go=((4, 256, HD), LOW),
    gqr=((ROWS, 512), LOW),
    a=((ROWS, D), F32),
    h=((ROWS, D), F32),
    n2=((ROWS, D), LOW),
    n2t=((D, ROWS), LOW),
    ga=((ROWS, FFH), F32),
    gb=((ROWS, FFH), F32),
    u=((ROWS, FFH), LOW),
    ggu=((ROWS, 2 * FFH), LOW),
    gf=((ROWS, D), LOW),
    gft=((D, ROWS), LOW),
    gal=((ROWS, D), LOW),
    gat=((D, ROWS), LOW),
    gh=((ROWS, D), F32),
    snd=((2, ROWS, D), LOW),
    rcv=((2, ROWS, D), LOW),
    gkv=((2, 1024, HD), F32),
    kvs=((1024, HD), LOW),
    kvr=((1024, HD), LOW),
    hs=((ROWS, HD), LOW),
    hr=((ROWS, HD), LOW),
    gkr=((ROWS, HD), LOW),
    final=((4, 80, WIRE), LOW),
    mine=((80, 256), F32),
    theirs=((80, 256), F32),
)


def layer_kernel(tok, seg_row, seg_col, cot, wq, wkv, wo, wgu, wd, ng, hg, out, igrad, grads, *rest):
    names = list(SCRATCH)
    g = types.SimpleNamespace(**dict(zip(names, rest[: len(names)])))
    rest = rest[len(names) :]
    bufs = (rest[0:5], rest[5:10])
    x, y, z = spot()
    core = lax.axis_index("tensor")
    mate = {"tensor": 1 - core}
    rings = (Ring("x", x, y), Ring("y", x, y))
    gather_wires = Wires(rest[10], rest[11])
    scatter_wires = Wires(rest[12], rest[13])
    other = Wires(rest[14], rest[15])
    greet(
        [r.to_f(k) for r in rings for k in (1, -1)]
        + [{"ctx": place(z + k)} for k in (1, 2, 3)]
        + [mate]
    )

    pieces = [
        [Gather(ring, gather_wires, g.wire, g.whole, *piece[i]) for i, ring in enumerate(rings)]
        for piece in GATHERS
    ]

    def step(part, name):
        for one in part:
            getattr(one, name)()

    p0, p1, p2, p3 = pieces

    g.pad[...] = jnp.zeros((1024, 128), F32)
    g.tall[...] = jnp.zeros((128, D), F32)
    g.wire[:, KV:QUERY] = fold(wkv[:, pl.ds(pl.multiple_of(core * HD, HD), HD)].astype(F32)).astype(LOW)
    g.wire[:, QUERY:EXTRA] = fold(wq[...].astype(F32)).astype(LOW)
    g.tall[0:4, 0:40] = ng[...].astype(F32)
    g.tall[0:2, 128:144] = hg[...].astype(F32)
    first = jnp.transpose(g.tall[:, 0:128])[:40]
    second = jnp.transpose(g.tall[:, 128:256])[:40]
    g.wire[:, EXTRA:OUT] = jnp.concatenate([first, second], axis=0).astype(LOW)
    step(p0, "one")
    g.whole[y, x, :, KV:OUT] = g.wire[:, KV:OUT]
    tok_wire = other.copy(tok, g.tokh, {"ctx": place(z + 1)})
    seg_wire = other.copy(seg_row, g.segp, {"ctx": place(z + 1)})
    g.pad[0:512, 0:40] = wo[...].astype(F32)
    g.wire[:, OUT:GATEUP] = fold(jnp.transpose(g.pad[0:512, :])[:40]).astype(LOW)
    step(p1, "one")
    g.whole[y, x, :, OUT:GATEUP] = g.wire[:, OUT:GATEUP]
    step(p0, "two")
    for i in range(2):
        g.wire[40 * i : 40 * i + 40, GATEUP:DOWN] = wgu[i]
    step(p2, "one")
    g.whole[y, x, :, GATEUP:DOWN] = g.wire[:, GATEUP:DOWN]
    step(p1, "two")
    step(p0, "three")
    g.pad[:, 0:40] = wd[...].astype(F32)
    g.wire[:, DOWN:WIRE] = fold(jnp.transpose(g.pad[...])[:40]).astype(LOW)
    step(p3, "one")
    g.whole[y, x, :, DOWN:WIRE] = g.wire[:, DOWN:WIRE]

    rates = jnp.exp(iota((1, 128), 1).astype(F32) * (-2.0 * math.log(10000.0) / HD))
    fine = iota((128, 128), 0).astype(F32) * rates
    fine_cos, fine_sin = jnp.cos(fine), jnp.sin(fine)
    coarse = (iota((8, 128), 0) * 128 + (z * ROWS - ROWS)).astype(F32) * rates
    coarse_cos, coarse_sin = jnp.cos(coarse), jnp.sin(coarse)
    for i in range(8):
        cc, cs = coarse_cos[i : i + 1], coarse_sin[i : i + 1]
        g.cos[128 * i : 128 * i + 128] = fine_cos * cc - fine_sin * cs
        g.sin[128 * i : 128 * i + 128] = fine_sin * cc + fine_cos * cs
    step(p1, "three")
    step(p2, "two")
    step(p0, "four")
    seg_wire.wait_recv()
    column = seg_col[...]
    below_prior = jnp.sum((g.segp[...] < column).astype(F32), axis=1, keepdims=True)
    below_prior = jnp.where(z == 0, float(ROWS), below_prior)
    below_own = jnp.sum((seg_row[...] < column).astype(F32), axis=1, keepdims=True)
    lowest = jnp.maximum(below_prior + below_own, iota((ROWS, 1), 0).astype(F32) + 1.0)
    lowest = jnp.broadcast_to(lowest, (ROWS, 128))
    g.lo_col[...] = lowest
    g.lo_row[...] = jnp.transpose(lowest)[0:8]
    g.dgains[...] = jnp.zeros((8, D), F32)
    g.dheads[...] = jnp.zeros((8, HD), F32)
    g.gkv[...] = jnp.zeros((2, 1024, HD), F32)
    step(p3, "two")
    step(p1, "four")
    step(p2, "three")

    def assemble(first, second, start, width, w=128):
        def one(i, carry):
            at = pl.multiple_of(i * w, w)
            block = g.whole[:, :, :, pl.ds(start + at, w)].astype(F32)
            first[:, pl.ds(at, w)] = block[:, :, :40].reshape(D, w).astype(LOW)
            if second is None:
                first[:, pl.ds(at + width, w)] = block[:, :, 40:].reshape(D, w).astype(LOW)
            else:
                second[:, pl.ds(at, w)] = block[:, :, 40:].reshape(D, w).astype(LOW)
            return carry

        lax.fori_loop(0, width // w, one, 0)

    step(p0, "finish")
    block = g.whole[:, :, :, EXTRA:OUT].astype(F32)
    g.gains[...] = jnp.transpose(block[:, :, :40].reshape(D, 128))[:8]
    spread_heads = jnp.transpose(block[:, :, 40:].reshape(D, 128))[:8]
    column_at, head_at = iota((D, HD), 0), iota((D, HD), 1)
    pick = (column_at == 40 * (head_at >> 4) + (head_at & 15)).astype(F32).astype(LOW)
    g.heads[...] = dot(spread_heads.astype(LOW), pick)
    assemble(g.wkv, None, KV, 128)
    assemble(g.wq, None, QUERY, 256)

    gain0, gain1, gain2, gain3 = (g.gains[i : i + 1] for i in range(4))
    qgain, kgain = g.heads[0:1], g.heads[1:2]

    def keys_of(start, normed):
        raw = dot(normed, g.wkv[...])
        at = slice(start, start + 256)
        if start >= ROWS:
            g.kvraw[start - ROWS : start - ROWS + 256] = raw
        turned = turn(raw * rms(raw) * kgain, g.cos[at], g.sin[at])
        g.kvb[core, at] = jnp.where(core == 0, turned, raw).astype(LOW)

    for i in range(2):
        block = tok[256 * i : 256 * i + 256].astype(F32)
        normed = block * rms(block) * gain0
        g.n1[ROWS + 256 * i : ROWS + 256 * i + 256] = normed.astype(LOW)
        g.n1t[:, 256 * i : 256 * i + 256] = jnp.transpose(normed).astype(LOW)
        keys_of(ROWS + 256 * i, normed.astype(LOW))
    own_kv = g.kvb.at[core, pl.ds(ROWS, ROWS)]
    own_wire = other.copy(own_kv, own_kv, mate)
    tok_wire.wait_recv()
    for i in range(2):
        block = g.tokh[256 * i : 256 * i + 256].astype(F32)
        keys_of(256 * i, (block * rms(block) * gain0).astype(LOW))
    prior_kv = g.kvb.at[core, pl.ds(0, ROWS)]
    prior_wire = other.copy(prior_kv, prior_kv, mate)
    for i in range(2):
        raw = dot(g.n1[ROWS + 256 * i : ROWS + 256 * i + 256], g.wq[...])
        at = slice(ROWS + 256 * i, ROWS + 256 * i + 256)
        for h in range(2):
            part = raw[:, HD * h : HD * h + HD]
            turned = turn(part * rms(part) * qgain, g.cos[at], g.sin[at]).astype(LOW)
            for j in range(2):
                g.qraw[2 * i + j, 128 * h : 128 * h + 128] = part[128 * j : 128 * j + 128]
                g.q[2 * i + j, 128 * h : 128 * h + 128] = turned[128 * j : 128 * j + 128]
    step(p3, "three")
    step(p2, "four")
    own_wire.wait_recv()
    prior_wire.wait_recv()

    def twice(block, axis):
        return jnp.concatenate([block, block], axis=axis)

    def attend(b, carry):
        start = pl.multiple_of(b * 128, 128)
        keys, values = g.kvb[0, pl.ds(start, D)], g.kvb[1, pl.ds(start, D)]
        scores = dot(g.q[b], keys, NT) * SCALE
        lowest = twice(g.lo_col[pl.ds(start, 128), 0:1], 0) - (b * 128).astype(F32)
        place_k = iota((256, D), 1).astype(F32)
        highest = (iota((256, 1), 0) & 127).astype(F32) + float(WINDOW)
        scores = jnp.where((place_k >= lowest) & (place_k <= highest), scores, -1e30)
        expo = jnp.exp(scores - jnp.max(scores, axis=-1, keepdims=True))
        probs = (expo / jnp.sum(expo, axis=-1, keepdims=True)).astype(LOW)
        mixed = dot(probs, values).astype(LOW)
        g.o[pl.ds(start, 128), 0:HD] = mixed[:128]
        g.o[pl.ds(start, 128), HD : 2 * HD] = mixed[128:]
        return carry

    lax.fori_loop(0, 4, attend, 0)
    step(p1, "finish")
    assemble(g.wo, None, OUT, 256)

    halves = [slice(0, 256), slice(256, 512)]

    def swap(number, rows, value):
        g.snd[number, rows] = value.astype(LOW)
        return other.copy(g.snd.at[number, rows], g.rcv.at[number, rows], mate)

    def total(number, rows):
        return g.snd[number, rows].astype(F32) + g.rcv[number, rows].astype(F32)

    sent = [swap(0, rows, dot(g.o[rows], g.wo[...], NT)) for rows in halves]
    step(p3, "four")
    for i, rows in enumerate(halves):
        sent[i].wait_recv()
        branch = total(0, rows)
        g.a[rows] = branch
        hidden = tok[rows].astype(F32) + branch * rms(branch) * gain1
        g.h[rows] = hidden
        normed = hidden * rms(hidden) * gain2
        g.n2[rows] = normed.astype(LOW)
        g.n2t[:, rows] = jnp.transpose(normed).astype(LOW)
    for made in sent:
        made.wait_send()
    step(p2, "finish")
    assemble(g.wg, g.wu, GATEUP, FFH)

    c0, c1 = math.sqrt(2.0 / math.pi), 0.044715

    def forward_ff(i, carry):
        at = pl.multiple_of(i * 256, 256)
        cols = pl.ds(at, 256)
        for rows in halves:
            gate = dot(g.n2[rows], g.wg[:, cols])
            up = dot(g.n2[rows], g.wu[:, cols])
            square = gate * gate
            t = jnp.tanh(c0 * gate * (1.0 + c1 * square))
            act = 0.5 * gate * (1.0 + t)
            slope = 0.5 * (1.0 + t) + 0.5 * gate * (1.0 - t * t) * (c0 * (1.0 + 3.0 * c1 * square))
            g.ga[rows, cols] = act
            g.gb[rows, cols] = up * slope
            g.u[rows, cols] = (act * up).astype(LOW)
        return carry

    lax.fori_loop(0, 4, forward_ff, 0)
    step(p3, "finish")
    gather_wires.drain()
    assemble(g.wd, None, DOWN, 512)

    sent = [swap(1, rows, dot(g.u[rows], g.wd[...], NT)) for rows in halves]
    for i, rows in enumerate(halves):
        sent[i].wait_recv()
        feed = total(1, rows)
        out[rows] = (g.h[rows] + feed * rms(feed) * gain3).astype(LOW)
        back, slope = norm_back(feed, gain3, cot[rows].astype(F32))
        g.dgains[3:4] += slope
        g.gf[rows] = back.astype(LOW)
        g.gft[:, rows] = jnp.transpose(back).astype(LOW)
    for made in sent:
        made.wait_send()

    def backward_ff(i, carry):
        at = pl.multiple_of(i * 256, 256)
        cols = pl.ds(at, 256)
        for rows in halves:
            inner = dot(g.gf[rows], g.wd[:, cols])
            g.ggu[rows, cols] = (inner * g.gb[rows, cols]).astype(LOW)
            g.ggu[rows, pl.ds(at + FFH, 256)] = (inner * g.ga[rows, cols]).astype(LOW)
        return carry

    lax.fori_loop(0, 4, backward_ff, 0)
    sent = [
        swap(
            0,
            rows,
            dot(g.ggu[rows, 0:FFH], g.wg[...], NT) + dot(g.ggu[rows, FFH:], g.wu[...], NT),
        )
        for rows in halves
    ]

    parts, offsets = [], [0, 0]
    for piece in SCATTERS:
        made = []
        for i, ring in enumerate(rings):
            if piece[i] is not None:
                start, width = piece[i]
                made.append(
                    Scatter(
                        ring, scatter_wires, g.whole, bufs[i], g.final, z, start, width, offsets[i]
                    )
                )
                offsets[i] += width
        parts.append(made)
    s0, s1, s2, s3, se = parts

    def put(left, right, start, begin, end, gap, w=256):
        def one(i, carry):
            at = pl.multiple_of(i * w, w)
            first = dot(left[...], right[:, pl.ds(at, w)]).reshape(16, 40, w)
            second = dot(left[...], right[:, pl.ds(at + gap, w)]).reshape(16, 40, w)
            block = jnp.concatenate([first, second], axis=1).astype(LOW)
            g.whole[:, :, :, pl.ds(start + at, w)] = block.reshape(4, 4, 80, w)
            return carry

        lax.fori_loop(begin // w, end // w, one, 0)

    put(g.gft, g.u, DOWN, 0, 512, 512)
    step(s3, "one")
    put(g.n2t, g.ggu, GATEUP, 0, 512, FFH)
    step(s2[:1], "one")
    step(s3, "two")
    put(g.n2t, g.ggu, GATEUP, 512, 1024, FFH)
    step(s2[1:], "one")
    for i, rows in enumerate(halves):
        sent[i].wait_recv()
        back, slope = norm_back(g.h[rows], gain2, total(0, rows))
        g.dgains[2:3] += slope
        hidden = cot[rows].astype(F32) + back
        g.gh[rows] = hidden
        back, slope = norm_back(g.a[rows], gain1, hidden)
        g.dgains[1:2] += slope
        low = back.astype(LOW)
        g.gat[:, rows] = jnp.transpose(back).astype(LOW)
        grad = dot(low, g.wo[...]).astype(LOW)
        for j in range(2):
            for h in range(2):
                g.go[2 * i + j, 128 * h : 128 * h + 128] = grad[
                    128 * j : 128 * j + 128, HD * h : HD * h + HD
                ]
    for made in sent:
        made.wait_send()
    step(s3, "three")
    step(s2[:1], "two")
    put(g.gat, g.o, OUT, 0, 256, 256)
    step(s1, "one")
    step(s2[1:], "two")

    def attend_back(b, carry):
        start = pl.multiple_of(b * 128, 128)
        keys, values = g.kvb[0, pl.ds(start, D)], g.kvb[1, pl.ds(start, D)]
        queries, grad = g.q[b], g.go[b]
        scores = dot(keys, queries, NT) * SCALE
        lowest = twice(g.lo_row[0:1, pl.ds(start, 128)], 1) - (b * 128).astype(F32)
        place_k = iota((D, 256), 0).astype(F32)
        highest = (iota((1, 256), 1) & 127).astype(F32) + float(WINDOW)
        scores = jnp.where((place_k >= lowest) & (place_k <= highest), scores, -1e30)
        expo = jnp.exp(scores - jnp.max(scores, axis=0, keepdims=True))
        probs = expo * (1.0 / jnp.sum(expo, axis=0, keepdims=True))
        grad_probs = dot(values, grad, NT)
        spread = jnp.sum(probs * grad_probs, axis=0, keepdims=True)
        grad_scores = (probs * (grad_probs - spread)).astype(LOW)
        g.gkv[0, pl.ds(start, D)] += dot(grad_scores, queries) * SCALE
        g.gkv[1, pl.ds(start, D)] += dot(probs.astype(LOW), grad)
        grad_q = dot(grad_scores, keys, TN) * SCALE
        at = pl.ds(pl.multiple_of(ROWS + start, 128), 128)
        grad_q = turn_back(grad_q, twice(g.cos[at], 0), twice(g.sin[at], 0))
        back, slope = norm_back(g.qraw[b], qgain, grad_q)
        g.dheads[0:1] += slope
        g.gqr[pl.ds(start, 128), 0:HD] = back[:128].astype(LOW)
        g.gqr[pl.ds(start, 128), HD : 2 * HD] = back[128:].astype(LOW)
        return carry

    lax.fori_loop(0, 2, attend_back, 0)
    step(s3, "four")
    step(s2[:1], "three")
    lax.fori_loop(2, 4, attend_back, 0)
    g.kvs[...] = g.gkv[1 - core].astype(LOW)
    kv_wire = other.copy(g.kvs, g.kvr, mate)
    step(s2[1:], "three")
    step(s1, "two")
    step(s3, "five")
    put(g.n1t, g.gqr, QUERY, 0, 256, 256)
    kv_wire.wait_recv()
    g.hs[...] = added(g.gkv[core, 0:ROWS], g.kvr[0:ROWS]).astype(LOW)
    halo_wire = other.copy(g.hs, g.hr, {"ctx": place(z - 1)})
    step(s2, "four")
    step(s1, "three")
    halo_wire.wait_recv()
    for i, rows in enumerate(halves):
        after = slice(ROWS + 256 * i, ROWS + 256 * i + 256)
        grad = added(g.gkv[core, after], g.kvr[after], g.hr[rows])
        back, slope = norm_back(g.kvraw[rows], kgain, turn_back(grad, g.cos[after], g.sin[after]))
        g.dheads[1:2] += jnp.where(core == 0, slope, 0.0)
        low = jnp.where(core == 0, back, grad).astype(LOW)
        g.gkr[rows] = low
    put(g.n1t, g.gkr, KV, 0, 128, 128, w=128)
    step(s0, "one")
    sent = [
        swap(1, rows, dot(g.gqr[rows], g.wq[...], NT) + dot(g.gkr[rows], g.wkv[...], NT))
        for rows in halves
    ]
    step(s2, "five")
    step(s1, "four")
    for i, rows in enumerate(halves):
        sent[i].wait_recv()
        back, slope = norm_back(tok[rows].astype(F32), gain0, total(1, rows))
        g.dgains[0:1] += slope
        igrad[rows] = g.gh[rows] + back
    g.tall[...] = jnp.zeros((128, D), F32)
    g.tall[0:8] = g.dgains[...]
    first = jnp.transpose(g.tall[...]).reshape(16, 40, 128)
    g.tall[0:8] = dot(g.dheads[...].astype(LOW), pick, NT)
    second = jnp.transpose(g.tall[...]).reshape(16, 40, 128)
    block = jnp.concatenate([first, second], axis=1).astype(LOW)
    g.whole[:, :, :, EXTRA:OUT] = block.reshape(4, 4, 80, 128)
    step(se, "one")
    step(s0, "two")
    step(s1, "five")
    step(se, "two")
    step(s0, "three")
    step(s3, "finish")

    def put_final(start, width):
        cols = pl.ds(start, width)
        return added(*(g.final[i, :, cols] for i in range(4)))

    grads[:, DOWN + 128 : WIRE + 128] = put_final(DOWN, 512)
    step(se, "three")
    step(s0, "four")
    step(s2, "finish")
    grads[:, GATEUP + 128 : DOWN + 128] = put_final(GATEUP, 1024)
    step(se, "four")
    step(s0, "five")
    step(s1, "finish")
    grads[:, OUT + 128 : GATEUP + 128] = put_final(OUT, 256)
    step(se, "five")
    step(s0, "finish")
    g.mine[:, 0:128] = put_final(KV, 128)
    grads[:, QUERY + 128 : EXTRA + 128] = put_final(QUERY, 256)
    step(se, "finish")
    ends = put_final(EXTRA, 128)
    g.mine[:, 128:256] = ends
    last_wire = other.copy(g.mine, g.theirs, mate)
    last_wire.wait_recv()
    own, far = g.mine[:, 0:128], g.theirs[:, 0:128]
    grads[:, 0:128] = jnp.where(core == 0, own, far)
    grads[:, 128:256] = jnp.where(core == 0, far, own)
    grads[0:40, EXTRA + 128 : OUT + 128] = ends[:40]
    grads[40:80, EXTRA + 128 : OUT + 128] = ends[40:] + g.theirs[40:80, 128:256]
    scatter_wires.drain()
    for made in (tok_wire, seg_wire, own_wire, prior_wire, kv_wire, halo_wire, last_wire, *sent):
        made.wait_send()


def vmem():
    return pl.BlockSpec(memory_space=pltpu.VMEM)


def ring_buffers():
    return [
        pltpu.VMEM((2, 2, 80, SET_COLS), LOW),
        pltpu.VMEM((2, 4, 80, SET_COLS), LOW),
        pltpu.VMEM((4, 80, SET_COLS), LOW),
        pltpu.VMEM((80, SET_COLS), LOW),
        pltpu.VMEM((2, 80, SET_COLS), LOW),
    ]


def shards(
    tokens, segments, cotangent, w_query, w_keyval, w_out, w_gateup, w_down, norm_gains, head_gains
):
    output, input_grad, done = pl.pallas_call(
        layer_kernel,
        out_shape=(
            jax.ShapeDtypeStruct((ROWS, D), LOW),
            jax.ShapeDtypeStruct((ROWS, D), F32),
            jax.ShapeDtypeStruct((80, WIRE + 128), F32),
        ),
        in_specs=[vmem()] * 11,
        out_specs=(vmem(),) * 3,
        scratch_shapes=[
            *(pltpu.VMEM(*shape) for shape in SCRATCH.values()),
            *ring_buffers(),
            *ring_buffers(),
            pltpu.SemaphoreType.DMA((64,)),
            pltpu.SemaphoreType.DMA((64,)),
            pltpu.SemaphoreType.DMA((99,)),
            pltpu.SemaphoreType.DMA((99,)),
            pltpu.SemaphoreType.DMA((16,)),
            pltpu.SemaphoreType.DMA((16,)),
        ],
        compiler_params=pltpu.CompilerParams(
            collective_id=0, has_side_effects=True, vmem_limit_bytes=VMEM_BYTES
        ),
    )(
        tokens[0],
        segments,
        segments.reshape(ROWS, 1),
        cotangent[0],
        w_query,
        w_keyval,
        w_out,
        w_gateup,
        w_down,
        norm_gains,
        head_gains,
    )
    kv, query, extra, wide, gateup, down = 0, 256, 512, 640, 896, 1920
    keyval = jnp.concatenate([unfold(done[:, 0:128]), unfold(done[:, 128:256])], axis=1)
    return (
        output[None],
        input_grad[None],
        unfold(done[:, query:extra]),
        keyval,
        unfold(done[:, wide:gateup]).T,
        done[:, gateup:down].reshape(2, 40, -1),
        unfold(done[:, down:]).T,
        done[:40, extra : extra + 4].T,
        done[40:56, extra : extra + 2].T,
    )


def solution(mesh):
    placed = (
        P("dp", "ctx", None),
        P("dp", "ctx"),
        P("dp", "ctx", None),
        P("dp", "tensor"),
        P("dp", None),
        P("tensor", "dp"),
        P(None, "dp", "tensor"),
        P("tensor", "dp"),
        P(None, "dp"),
        P(None, "dp"),
    )
    return jax.shard_map(
        shards,
        mesh=mesh,
        in_specs=placed,
        out_specs=(
            P("dp", "ctx", None),
            P("dp", "ctx", None),
            P("dp", "tensor"),
            P("dp", None),
            P("tensor", "dp"),
            P(None, "dp", "tensor"),
            P("tensor", "dp"),
            P(None, "dp"),
            P(None, "dp"),
        ),
        check_vma=False,
    )
```

profile of v0, /device:TPU:1, one launch (start us, length us, event | category | flops | bytes accessed | tf_op | source)
XLA Modules:
  0.0 135.8 jit_solution(17216334303778477618)
XLA Ops:
  0.6 1.5 %copy.23.seg_col = s32[512,1]{1,0:T(8,128)} copy(s32[512,1]{0,1:T(1,128)} %bitcast.19) | data formatting | bytes 4096 | tf_op jit(solution)/shard_map/reshape | solution.py:793
  2.2 1.7 %copy.25.wd = bf16[1024,40]{1,0:T(8,128)(2,1)} copy(bf16[1024,40]{0,1:T(8,128)(2,1)} %param.17) | data formatting | bytes 163840 | tf_op args[7]
  3.9 1.5 %copy.24.wo = bf16[512,40]{1,0:T(8,128)(2,1)} copy(bf16[512,40]{0,1:T(8,128)(2,1)} %param.15) | data formatting | bytes 81920 | tf_op args[5]
  5.4 119.3 %shard_map.169 = (bf16[512,640]{1,0:T(8,128)(2,1)}, f32[512,640]{1,0:T(8,128)}, f32[80,2432]{1,0:T(8,128)}) custom-call(bf16[512,640]{1,0:T(8,128)(2,1)} %bitcast.16, s32[1,512]{1,0:T(1,128)} %seg_row.1, s32[512,1]{1,0:T(8,128)} %copy.23.seg_col, bf16[512,640]{1,0:T(8,128)(2,1)} %bitcast.17, bf16[40,512]{1,0:T(8,128)(2,1)} %wq.1, bf16[40,512]{1,0:T(8,128)(2,1)} %wkv.1, ...), custom_call_target="tpu_custom_call" | custom-call | tf_op jit(solution)/shard_map/pallas_call | solution.py:767
  124.7 0.0 copy-start.1
  124.7 0.9 fusion.1
  125.7 0.7 pad_maximum_fusion
  126.3 0.8 fusion.2
  127.1 0.6 pad_maximum_fusion.1
  127.8 0.0 copy-start
  127.8 1.0 fusion
  128.8 0.7 maximum_bitcast_fusion
  129.5 1.7 %slice.62 = f32[80,1024]{1,0:T(8,128)} slice(f32[80,2432]{1,0:T(8,128)} %get-tuple-element.14), slice={[0:80], [896:1920]} | slice | bytes 655360 | tf_op jit(solution)/shard_map/slice | solution.py:811
  131.2 0.7 slice_bitcast_fusion
  131.9 0.7 copy.26
  132.6 0.7 slice_bitcast_fusion.1
  133.3 0.6 copy.27
  133.9 0.0 copy-done.1
  133.9 0.8 copy.30
  134.8 0.0 copy-done
  134.8 1.1 copy.31
Async XLA Ops:
  124.7 9.2 %copy-start.1 = (bf16[512,640]{1,0:T(8,128)(2,1)S(1)}, bf16[512,640]{1,0:T(8,128)(2,1)}, u32[]{:S(2)}) copy-start(bf16[512,640]{1,0:T(8,128)(2,1)} %get-tuple-element.12) | copy-start | bytes 1966084
  127.8 7.0 %copy-start = (f32[512,640]{1,0:T(8,128)S(1)}, f32[512,640]{1,0:T(8,128)}, u32[]{:S(2)}) copy-start(f32[512,640]{1,0:T(8,128)} %get-tuple-element.13) | copy-start | bytes 3932164
where the time goes:
time: 136 us
  Pallas kernels  119 us (88%)
  local copies, waits for them, and re-layouts  13.9 us (10%)
  other arithmetic  2 us (1%)
    pallas_call x1, Pallas kernels, shards(): pl.pallas_call(layer_kernel, out_shape=(jax.ShapeDtypeStruct((ROWS, D), L...  119 us
    unnamed x10, local copies, waits for them, and re-layouts  6.46 us
    slice x3, local copies, waits for them, and re-layouts, unfold(): block[..., :rows, :]  2.75 us

commit v1 on v0

--- a/solution.py
+++ b/solution.py
@@ -139,11 +139,12 @@
 
 
 class Scatter:
-    def __init__(self, ring, wires, grads, bufs, final, z, start, width, offset):
+    def __init__(self, ring, wires, grads, bufs, final, z, start, width, offset, far):
         self.ring, self.wires, self.grads, self.final, self.z = ring, wires, grads, final, z
         self.r1, self.r2, self.sums, self.r3, self.r4 = bufs
         self.cols = pl.ds(start, width)
         self.near = pl.ds(offset, width)
+        self.far, self.start = far, start
 
     def one(self):
         r, c, n = self.ring, self.cols, self.near
@@ -220,17 +221,13 @@
         ).astype(jnp.bfloat16)
         part = self.final.at[self.z, :, c]
         self.zs = [self.wires.copy(part, part, {"ctx": place(self.z + k)}) for k in (1, 3, 2)]
+        if self.far is not None:
+            part = self.final.at[self.z, :, pl.ds(self.start, 128)]
+            self.zs += [self.wires.copy(part, self.far[0], target) for target in self.far[1]]
 
     def finish(self):
         for made in self.zs:
             made.wait_recv()
-
-
-def greet(targets):
-    barrier = pltpu.get_barrier_semaphore()
-    for target in targets:
-        pl.semaphore_signal(barrier, inc=1, device_id=target, device_id_type=MESH)
-    pl.semaphore_wait(barrier, len(targets))
 
 
 def spot():
@@ -281,7 +278,6 @@
 SCRATCH = dict(
     wire=((80, WIRE), LOW),
     whole=((4, 4, 80, WIRE), LOW),
-    pad=((1024, 128), F32),
     tall=((128, D), F32),
     wq=((D, 512), LOW),
     wkv=((D, HD), LOW),
@@ -330,12 +326,11 @@
     hr=((ROWS, HD), LOW),
     gkr=((ROWS, HD), LOW),
     final=((4, 80, WIRE), LOW),
-    mine=((80, 256), F32),
-    theirs=((80, 256), F32),
+    far=((4, 80, 256), LOW),
 )
 
 
-def layer_kernel(tok, seg_row, seg_col, cot, wq, wkv, wo, wgu, wd, ng, hg, out, igrad, grads, *rest):
+def layer_kernel(tok, seg_row, cot, wq, wkv, wo, wgu, wd, ng, hg, out, igrad, grads, *rest):
     names = list(SCRATCH)
     g = types.SimpleNamespace(**dict(zip(names, rest[: len(names)])))
     rest = rest[len(names) :]
@@ -347,11 +342,14 @@
     gather_wires = Wires(rest[10], rest[11])
     scatter_wires = Wires(rest[12], rest[13])
     other = Wires(rest[14], rest[15])
-    greet(
+    targets = (
         [r.to_f(k) for r in rings for k in (1, -1)]
         + [{"ctx": place(z + k)} for k in (1, 2, 3)]
-        + [mate]
+        + [{"ctx": place(z + k), "tensor": 1 - core} for k in range(4)]
     )
+    barrier = pltpu.get_barrier_semaphore()
+    for target in targets:
+        pl.semaphore_signal(barrier, inc=1, device_id=target, device_id_type=MESH)
 
     pieces = [
         [Gather(ring, gather_wires, g.wire, g.whole, *piece[i]) for i, ring in enumerate(rings)]
@@ -364,7 +362,6 @@
 
     p0, p1, p2, p3 = pieces
 
-    g.pad[...] = jnp.zeros((1024, 128), F32)
     g.tall[...] = jnp.zeros((128, D), F32)
     g.wire[:, KV:QUERY] = fold(wkv[:, pl.ds(pl.multiple_of(core * HD, HD), HD)].astype(F32)).astype(LOW)
     g.wire[:, QUERY:EXTRA] = fold(wq[...].astype(F32)).astype(LOW)
@@ -373,25 +370,21 @@
     first = jnp.transpose(g.tall[:, 0:128])[:40]
     second = jnp.transpose(g.tall[:, 128:256])[:40]
     g.wire[:, EXTRA:OUT] = jnp.concatenate([first, second], axis=0).astype(LOW)
+    pl.semaphore_wait(barrier, len(targets))
     step(p0, "one")
-    g.whole[y, x, :, KV:OUT] = g.wire[:, KV:OUT]
+    seg_wire = other.copy(seg_row, g.segp, {"ctx": place(z + 1)})
+    g.wire[:, OUT:GATEUP] = fold(wo[...].astype(F32)).astype(LOW)
+    step(p1, "one")
     tok_wire = other.copy(tok, g.tokh, {"ctx": place(z + 1)})
-    seg_wire = other.copy(seg_row, g.segp, {"ctx": place(z + 1)})
-    g.pad[0:512, 0:40] = wo[...].astype(F32)
-    g.wire[:, OUT:GATEUP] = fold(jnp.transpose(g.pad[0:512, :])[:40]).astype(LOW)
-    step(p1, "one")
-    g.whole[y, x, :, OUT:GATEUP] = g.wire[:, OUT:GATEUP]
+    g.whole[y, x, :, KV:GATEUP] = g.wire[:, KV:GATEUP]
+    g.wire[:, GATEUP:DOWN] = jnp.concatenate([wgu[0].astype(F32), wgu[1].astype(F32)], axis=0).astype(LOW)
     step(p0, "two")
-    for i in range(2):
-        g.wire[40 * i : 40 * i + 40, GATEUP:DOWN] = wgu[i]
     step(p2, "one")
-    g.whole[y, x, :, GATEUP:DOWN] = g.wire[:, GATEUP:DOWN]
     step(p1, "two")
     step(p0, "three")
-    g.pad[:, 0:40] = wd[...].astype(F32)
-    g.wire[:, DOWN:WIRE] = fold(jnp.transpose(g.pad[...])[:40]).astype(LOW)
+    g.wire[:, DOWN:WIRE] = fold(wd[...].astype(F32)).astype(LOW)
     step(p3, "one")
-    g.whole[y, x, :, DOWN:WIRE] = g.wire[:, DOWN:WIRE]
+    g.whole[y, x, :, GATEUP:WIRE] = g.wire[:, GATEUP:WIRE]
 
     rates = jnp.exp(iota((1, 128), 1).astype(F32) * (-2.0 * math.log(10000.0) / HD))
     fine = iota((128, 128), 0).astype(F32) * rates
@@ -406,10 +399,11 @@
     step(p2, "two")
     step(p0, "four")
     seg_wire.wait_recv()
-    column = seg_col[...]
-    below_prior = jnp.sum((g.segp[...] < column).astype(F32), axis=1, keepdims=True)
+    own_ids, prior_ids = seg_row[...].astype(F32), g.segp[...].astype(F32)
+    column = jnp.transpose(jnp.broadcast_to(own_ids, (128, ROWS)))[:, 0:1]
+    below_prior = jnp.sum((prior_ids < column).astype(F32), axis=1, keepdims=True)
     below_prior = jnp.where(z == 0, float(ROWS), below_prior)
-    below_own = jnp.sum((seg_row[...] < column).astype(F32), axis=1, keepdims=True)
+    below_own = jnp.sum((own_ids < column).astype(F32), axis=1, keepdims=True)
     lowest = jnp.maximum(below_prior + below_own, iota((ROWS, 1), 0).astype(F32) + 1.0)
     lowest = jnp.broadcast_to(lowest, (ROWS, 128))
     g.lo_col[...] = lowest
@@ -479,7 +473,6 @@
                 g.qraw[2 * i + j, 128 * h : 128 * h + 128] = part[128 * j : 128 * j + 128]
                 g.q[2 * i + j, 128 * h : 128 * h + 128] = turned[128 * j : 128 * j + 128]
     step(p3, "three")
-    step(p2, "four")
     own_wire.wait_recv()
     prior_wire.wait_recv()
 
@@ -502,6 +495,7 @@
         return carry
 
     lax.fori_loop(0, 4, attend, 0)
+    step(p2, "four")
     step(p1, "finish")
     assemble(g.wo, None, OUT, 256)
 
@@ -515,7 +509,6 @@
         return g.snd[number, rows].astype(F32) + g.rcv[number, rows].astype(F32)
 
     sent = [swap(0, rows, dot(g.o[rows], g.wo[...], NT)) for rows in halves]
-    step(p3, "four")
     for i, rows in enumerate(halves):
         sent[i].wait_recv()
         branch = total(0, rows)
@@ -527,6 +520,7 @@
         g.n2t[:, rows] = jnp.transpose(normed).astype(LOW)
     for made in sent:
         made.wait_send()
+    step(p3, "four")
     step(p2, "finish")
     assemble(g.wg, g.wu, GATEUP, FFH)
 
@@ -564,6 +558,43 @@
     for made in sent:
         made.wait_send()
 
+    def cross(start):
+        if start not in (KV, EXTRA):
+            return None
+        at = 0 if start == KV else 128
+        return g.far.at[z, :, pl.ds(at, 128)], [
+            {"ctx": place(z + k), "tensor": 1 - core} for k in range(4)
+        ]
+
+    parts, offsets = [], [0, 0]
+    for piece in SCATTERS:
+        made = []
+        for i, ring in enumerate(rings):
+            if piece[i] is not None:
+                start, width = piece[i]
+                made.append(
+                    Scatter(
+                        ring, scatter_wires, g.whole, bufs[i], g.final, z, start, width, offsets[i], cross(start)
+                    )
+                )
+                offsets[i] += width
+        parts.append(made)
+    s0, s1, s2, s3, se = parts
+
+    def put(left, right, start, begin, end, gap, w=256):
+        def one(i, carry):
+            at = pl.multiple_of(i * w, w)
+            first = dot(left[...], right[:, pl.ds(at, w)]).reshape(16, 40, w)
+            second = dot(left[...], right[:, pl.ds(at + gap, w)]).reshape(16, 40, w)
+            block = jnp.concatenate([first, second], axis=1).astype(LOW)
+            g.whole[:, :, :, pl.ds(start + at, w)] = block.reshape(4, 4, 80, w)
+            return carry
+
+        lax.fori_loop(begin // w, end // w, one, 0)
+
+    put(g.gft, g.u, DOWN, 0, 512, 512)
+    step(s3, "one")
+
     def backward_ff(i, carry):
         at = pl.multiple_of(i * 256, 256)
         cols = pl.ds(at, 256)
@@ -574,6 +605,7 @@
         return carry
 
     lax.fori_loop(0, 4, backward_ff, 0)
+    step(s3, "two")
     sent = [
         swap(
             0,
@@ -583,37 +615,8 @@
         for rows in halves
     ]
 
-    parts, offsets = [], [0, 0]
-    for piece in SCATTERS:
-        made = []
-        for i, ring in enumerate(rings):
-            if piece[i] is not None:
-                start, width = piece[i]
-                made.append(
-                    Scatter(
-                        ring, scatter_wires, g.whole, bufs[i], g.final, z, start, width, offsets[i]
-                    )
-                )
-                offsets[i] += width
-        parts.append(made)
-    s0, s1, s2, s3, se = parts
-
-    def put(left, right, start, begin, end, gap, w=256):
-        def one(i, carry):
-            at = pl.multiple_of(i * w, w)
-            first = dot(left[...], right[:, pl.ds(at, w)]).reshape(16, 40, w)
-            second = dot(left[...], right[:, pl.ds(at + gap, w)]).reshape(16, 40, w)
-            block = jnp.concatenate([first, second], axis=1).astype(LOW)
-            g.whole[:, :, :, pl.ds(start + at, w)] = block.reshape(4, 4, 80, w)
-            return carry
-
-        lax.fori_loop(begin // w, end // w, one, 0)
-
-    put(g.gft, g.u, DOWN, 0, 512, 512)
-    step(s3, "one")
     put(g.n2t, g.ggu, GATEUP, 0, 512, FFH)
     step(s2[:1], "one")
-    step(s3, "two")
     put(g.n2t, g.ggu, GATEUP, 512, 1024, FFH)
     step(s2[1:], "one")
     for i, rows in enumerate(halves):
@@ -635,10 +638,8 @@
     for made in sent:
         made.wait_send()
     step(s3, "three")
-    step(s2[:1], "two")
     put(g.gat, g.o, OUT, 0, 256, 256)
     step(s1, "one")
-    step(s2[1:], "two")
 
     def attend_back(b, carry):
         start = pl.multiple_of(b * 128, 128)
@@ -665,20 +666,19 @@
         g.gqr[pl.ds(start, 128), HD : 2 * HD] = back[128:].astype(LOW)
         return carry
 
-    lax.fori_loop(0, 2, attend_back, 0)
+    lax.fori_loop(0, 1, attend_back, 0)
+    step(s2, "two")
+    lax.fori_loop(1, 3, attend_back, 0)
     step(s3, "four")
-    step(s2[:1], "three")
-    lax.fori_loop(2, 4, attend_back, 0)
+    step(s1, "two")
+    lax.fori_loop(3, 4, attend_back, 0)
     g.kvs[...] = g.gkv[1 - core].astype(LOW)
     kv_wire = other.copy(g.kvs, g.kvr, mate)
-    step(s2[1:], "three")
-    step(s1, "two")
     step(s3, "five")
     put(g.n1t, g.gqr, QUERY, 0, 256, 256)
     kv_wire.wait_recv()
     g.hs[...] = added(g.gkv[core, 0:ROWS], g.kvr[0:ROWS]).astype(LOW)
     halo_wire = other.copy(g.hs, g.hr, {"ctx": place(z - 1)})
-    step(s2, "four")
     step(s1, "three")
     halo_wire.wait_recv()
     for i, rows in enumerate(halves):
@@ -694,7 +694,8 @@
         swap(1, rows, dot(g.gqr[rows], g.wq[...], NT) + dot(g.gkr[rows], g.wkv[...], NT))
         for rows in halves
     ]
-    step(s2, "five")
+    step(s2, "three")
+    step(s0, "two")
     step(s1, "four")
     for i, rows in enumerate(halves):
         sent[i].wait_recv()
@@ -709,42 +710,61 @@
     block = jnp.concatenate([first, second], axis=1).astype(LOW)
     g.whole[:, :, :, EXTRA:OUT] = block.reshape(4, 4, 80, 128)
     step(se, "one")
-    step(s0, "two")
+    step(s2, "four")
+    step(s0, "three")
+    step(se, "two")
     step(s1, "five")
-    step(se, "two")
-    step(s0, "three")
+    step(s2, "five")
+    step(s0, "four")
+    step(se, "three")
+    step(s0, "five")
+    step(se, "four")
+
+    def put_final(start, width, source=None):
+        cols = pl.ds(start, width)
+        return added(*((g.final if source is None else source)[i, :, cols] for i in range(4)))
+
     step(s3, "finish")
-
-    def put_final(start, width):
-        cols = pl.ds(start, width)
-        return added(*(g.final[i, :, cols] for i in range(4)))
-
     grads[:, DOWN + 128 : WIRE + 128] = put_final(DOWN, 512)
-    step(se, "three")
-    step(s0, "four")
-    step(s2, "finish")
-    grads[:, GATEUP + 128 : DOWN + 128] = put_final(GATEUP, 1024)
-    step(se, "four")
-    step(s0, "five")
     step(s1, "finish")
     grads[:, OUT + 128 : GATEUP + 128] = put_final(OUT, 256)
     step(se, "five")
+    step(s2, "finish")
+    grads[:, GATEUP + 128 : DOWN + 128] = put_final(GATEUP, 1024)
     step(s0, "finish")
-    g.mine[:, 0:128] = put_final(KV, 128)
+    own, far = put_final(KV, 128), put_final(0, 128, g.far)
+    grads[:, 0:128] = jnp.where(core == 0, own, far)
+    grads[:, 128:256] = jnp.where(core == 0, far, own)
     grads[:, QUERY + 128 : EXTRA + 128] = put_final(QUERY, 256)
     step(se, "finish")
-    ends = put_final(EXTRA, 128)
-    g.mine[:, 128:256] = ends
-    last_wire = other.copy(g.mine, g.theirs, mate)
-    last_wire.wait_recv()
-    own, far = g.mine[:, 0:128], g.theirs[:, 0:128]
-    grads[:, 0:128] = jnp.where(core == 0, own, far)
-    grads[:, 128:256] = jnp.where(core == 0, far, own)
-    grads[0:40, EXTRA + 128 : OUT + 128] = ends[:40]
-    grads[40:80, EXTRA + 128 : OUT + 128] = ends[40:] + g.theirs[40:80, 128:256]
+    own, far = put_final(EXTRA, 128), put_final(128, 128, g.far)
+    grads[0:40, EXTRA + 128 : OUT + 128] = own[:40]
+    grads[40:80, EXTRA + 128 : OUT + 128] = own[40:] + far[40:]
     scatter_wires.drain()
-    for made in (tok_wire, seg_wire, own_wire, prior_wire, kv_wire, halo_wire, last_wire, *sent):
+    for made in (tok_wire, seg_wire, own_wire, prior_wire, kv_wire, halo_wire, *sent):
         made.wait_send()
+
+
+def hand_out(output, input_grad, done, out, igrad, query, keyval, wide, gateup, down, norms, heads, sems):
+    copies = [
+        pltpu.make_async_copy(output, out, sems.at[0]),
+        pltpu.make_async_copy(input_grad, igrad, sems.at[1]),
+    ]
+    for made in copies:
+        made.start()
+    keyval[:, 0:256] = unfold(done[:, 0:128])
+    keyval[:, 256:512] = unfold(done[:, 128:256])
+    query[...] = unfold(done[:, 256:512])
+    wide[...] = unfold(done[:, 640:896])
+    gateup[0] = done[:40, 896:1920]
+    gateup[1] = done[40:, 896:1920]
+    down[...] = unfold(done[:, 1920:])
+    square = jnp.concatenate([done[:, 512:640], jnp.zeros((48, 128), F32)], axis=0)
+    turned = jnp.transpose(square)
+    norms[...] = turned[:4, :40]
+    heads[...] = turned[:2, 40:56]
+    for made in copies:
+        made.wait()
 
 
 def vmem():
@@ -771,7 +791,7 @@
             jax.ShapeDtypeStruct((ROWS, D), F32),
             jax.ShapeDtypeStruct((80, WIRE + 128), F32),
         ),
-        in_specs=[vmem()] * 11,
+        in_specs=[vmem()] * 10,
         out_specs=(vmem(),) * 3,
         scratch_shapes=[
             *(pltpu.VMEM(*shape) for shape in SCRATCH.values()),
@@ -779,8 +799,8 @@
             *ring_buffers(),
             pltpu.SemaphoreType.DMA((64,)),
             pltpu.SemaphoreType.DMA((64,)),
-            pltpu.SemaphoreType.DMA((99,)),
-            pltpu.SemaphoreType.DMA((99,)),
+            pltpu.SemaphoreType.DMA((112,)),
+            pltpu.SemaphoreType.DMA((112,)),
             pltpu.SemaphoreType.DMA((16,)),
             pltpu.SemaphoreType.DMA((16,)),
         ],
@@ -790,28 +810,44 @@
     )(
         tokens[0],
         segments,
-        segments.reshape(ROWS, 1),
         cotangent[0],
         w_query,
         w_keyval,
-        w_out,
+        w_out.T,
         w_gateup,
-        w_down,
+        w_down.T,
         norm_gains,
         head_gains,
     )
-    kv, query, extra, wide, gateup, down = 0, 256, 512, 640, 896, 1920
-    keyval = jnp.concatenate([unfold(done[:, 0:128]), unfold(done[:, 128:256])], axis=1)
+    whole = pl.BlockSpec(memory_space=pl.ANY)
+    results = pl.pallas_call(
+        hand_out,
+        out_shape=(
+            jax.ShapeDtypeStruct((ROWS, D), LOW),
+            jax.ShapeDtypeStruct((ROWS, D), F32),
+            jax.ShapeDtypeStruct((40, 512), F32),
+            jax.ShapeDtypeStruct((40, 512), F32),
+            jax.ShapeDtypeStruct((40, 512), F32),
+            jax.ShapeDtypeStruct((2, 40, FFH), F32),
+            jax.ShapeDtypeStruct((40, FFH), F32),
+            jax.ShapeDtypeStruct((4, 40), F32),
+            jax.ShapeDtypeStruct((2, 16), F32),
+        ),
+        in_specs=[whole, whole, vmem()],
+        out_specs=(whole, whole) + (vmem(),) * 7,
+        scratch_shapes=[pltpu.SemaphoreType.DMA((2,))],
+        compiler_params=pltpu.CompilerParams(vmem_limit_bytes=16 * 1024 * 1024),
+    )(output, input_grad, done)
     return (
-        output[None],
-        input_grad[None],
-        unfold(done[:, query:extra]),
-        keyval,
-        unfold(done[:, wide:gateup]).T,
-        done[:, gateup:down].reshape(2, 40, -1),
-        unfold(done[:, down:]).T,
-        done[:40, extra : extra + 4].T,
-        done[40:56, extra : extra + 2].T,
+        results[0][None],
+        results[1][None],
+        results[2],
+        results[3],
+        results[4].T,
+        results[5],
+        results[6].T,
+        results[7],
+        results[8],
     )
 
 

time: 136 us -> 122 us (0.90)
  local copies, waits for them, and re-layouts: 13.9 us -> 3.53 us
  other arithmetic: 2 us -> 0 us
    slice x4 -> x0, local copies, waits for them, and re-layouts: 4.47 us -> none  [the longest x3 2.75 us: unfold(): block[..., :rows, :]]
    pallas_call x1, Pallas kernels: 119 us -> 115 us  [shards(): pl.pallas_call(layer_kernel, out_shape=(jax.ShapeDtypeStruct((ROWS, D), L...]
    unnamed x10 -> x6, local copies, waits for them, and re-layouts: 6.46 us -> 3.53 us
    pallas_call x0 -> x1, Pallas kernels: none -> 2.15 us  [shards(): pl.pallas_call(hand_out, out_shape=(jax.ShapeDtypeStruct((ROWS, D), LOW),...]
    reshape x1 -> x0, local copies, waits for them, and re-layouts: 1.54 us -> none  [shards(): segments.reshape(ROWS, 1)]
    transpose x2 -> x0, local copies, waits for them, and re-layouts: 1.43 us -> none  [the longest x1 0.73 us: shards(): done[:40, extra:extra + 4]]
where the time goes in v1:
time: 122 us
  Pallas kernels  118 us (97%)
  local copies, waits for them, and re-layouts  3.53 us (3%)
    pallas_call x1, Pallas kernels, shards(): pl.pallas_call(layer_kernel, out_shape=(jax.ShapeDtypeStruct((ROWS, D), L...  115 us
    unnamed x6, local copies, waits for them, and re-layouts  3.53 us

profile of v1, /device:TPU:1, one launch (start us, length us, event | category | flops | bytes accessed | tf_op | source)
XLA Modules:
  0.0 122.0 jit_solution(14861938628436011264)
XLA Ops:
  0.6 115.5 %shard_map.169 = (bf16[512,640]{1,0:T(8,128)(2,1)}, f32[512,640]{1,0:T(8,128)}, f32[80,2432]{1,0:T(8,128)}) custom-call(bf16[512,640]{1,0:T(8,128)(2,1)} %bitcast.8, s32[1,512]{1,0:T(1,128)} %seg_row.1, bf16[512,640]{1,0:T(8,128)(2,1)} %bitcast.9, bf16[40,512]{1,0:T(8,128)(2,1)} %wq.1, bf16[40,512]{1,0:T(8,128)(2,1)} %wkv.1, bf16[40,512]{1,0:T(8,128)(2,1)} %bitcast.11, ...), custom_call_target="tpu_custom_call" | custom-call | tf_op jit(solution)/shard_map/pallas_call | solution.py:787
  116.1 0.0 copy-start
  116.1 1.3 %copy-done = f32[512,640]{1,0:T(8,128)S(1)} copy-done((f32[512,640]{1,0:T(8,128)S(1)}, f32[512,640]{1,0:T(8,128)}, u32[]{:S(2)}) %copy-start) | copy-done | bytes 1310744
  117.4 0.0 copy-start.1
  117.4 1.1 copy-done.1
  118.6 0.0 copy-start.2
  118.6 1.1 copy-done.2
  119.6 2.1 %shard_map.170 = (bf16[512,640]{1,0:T(8,128)(2,1)}, f32[512,640]{1,0:T(8,128)}, f32[40,512]{1,0:T(8,128)}, f32[40,512]{1,0:T(8,128)}, f32[40,512]{1,0:T(8,128)},...) custom-call(bf16[512,640]{1,0:T(8,128)(2,1)S(1)} %copy-done.2, ...), custom_call_target="tpu_custom_call" | custom-call | tf_op jit(solution)/shard_map/pallas_call | solution.py:823
Async XLA Ops:
  116.1 1.3 %copy-start = (f32[512,640]{1,0:T(8,128)S(1)}, f32[512,640]{1,0:T(8,128)}, u32[]{:S(2)}) copy-start(f32[512,640]{1,0:T(8,128)} %get-tuple-element.22.input_grad) | copy-start | bytes 3932164
  117.4 1.1 copy-start.1
  118.6 1.1 copy-start.2

commit v2 on v1

v2 whole, which is shorter than its diff:
```python
import math
import types

import jax
import jax.numpy as jnp
from jax import lax
from jax.experimental import pallas as pl
from jax.experimental.pallas import tpu as pltpu
from jax.sharding import PartitionSpec as P

WINDOW = 512
EPSILON = 1e-06
MESH = pl.DeviceIdType.MESH
VMEM_BYTES = 60 * 1024 * 1024

KV, QUERY, EXTRA, OUT, GATEUP, DOWN, WIRE = 0, 128, 384, 512, 768, 1792, 2304
GATHERS = (
    ((0, 256), (256, 256)),
    ((512, 128), (640, 128)),
    ((768, 512), (1280, 512)),
    ((1792, 256), (2048, 256)),
)
SCATTERS = (
    ("s3", (1792, 256), (2048, 256)),
    ("sa", (768, 256), (1024, 256)),
    ("sb", (1280, 256), (1536, 256)),
    ("s1", (512, 128), (640, 128)),
    ("s0", (0, 256), (256, 128)),
)
SET_COLS = (1152, 1024)
CUT = 48
ROWS, D, HD, FFH = 512, 640, 256, 1024
SCALE = 1.0 / math.sqrt(HD)
LOW = jnp.bfloat16
F32 = jnp.float32
NN, NT, TN = ((1,), (0,)), ((1,), (1,)), ((0,), (0,))


def place(u):
    return lax.rem(u + 8, 4)


class Wires:
    def __init__(self, send, recv):
        self.send, self.recv, self.used = send, recv, 0
        self.started = []

    def copy(self, src, dst, target):
        index = self.used
        self.used += 1
        made = pltpu.make_async_remote_copy(
            src_ref=src,
            dst_ref=dst,
            send_sem=self.send.at[index],
            recv_sem=self.recv.at[index],
            device_id=target,
            device_id_type=MESH,
        )
        made.start()
        self.started.append(made)
        return made

    def drain(self):
        for made in self.started:
            made.wait_send()
        self.started = []


class Ring:
    def __init__(self, first, x, y):
        self.first = first
        self.f, self.s = (x, y) if first == "x" else (y, x)

    def slot(self, ref, f, s, *rest):
        return ref.at[(s, f) + rest] if self.first == "x" else ref.at[(f, s) + rest]

    def index(self, f, s):
        return (s, f) if self.first == "x" else (f, s)

    def to_f(self, step):
        f = place(self.f + step)
        return {"dp": self.s * 4 + f} if self.first == "x" else {"dp": f * 4 + self.s}

    def to_s(self, step):
        s = place(self.s + step)
        return {"dp": s * 4 + self.f} if self.first == "x" else {"dp": self.f * 4 + s}


class Gather:
    def __init__(self, ring, wires, shard, whole, direct, start, width):
        self.ring, self.wires, self.shard, self.whole = ring, wires, shard, whole
        self.direct = direct
        self.cols = pl.ds(start, width)

    def one(self):
        r, c = self.ring, self.cols
        src = self.shard.at[:, c]
        dst = r.slot(self.whole, r.f, r.s, slice(None), c)
        self.a = self.wires.copy(src, dst, r.to_f(1))
        self.b = self.wires.copy(src, dst, r.to_f(-1))
        if self.direct:
            self.c = self.wires.copy(src, dst, r.to_f(2))

    def two(self):
        r, c = self.ring, self.cols
        self.a.wait_recv()
        part = r.slot(self.whole, place(r.f - 1), r.s, pl.ds(0, CUT), c)
        a = self.wires.copy(part, part, r.to_f(1))
        self.b.wait_recv()
        part = r.slot(self.whole, place(r.f + 1), r.s, pl.ds(CUT, 80 - CUT), c)
        b = self.wires.copy(part, part, r.to_f(-1))
        self.a, self.b = a, b

    def three(self):
        r, c = self.ring, self.cols
        self.a.wait_recv()
        self.b.wait_recv()
        if self.direct:
            self.c.wait_recv()
        part = r.slot(self.whole, slice(None), r.s, slice(None), c)
        self.a = self.wires.copy(part, part, r.to_s(1))
        self.b = self.wires.copy(part, part, r.to_s(-1))

    def four(self):
        r, c = self.ring, self.cols
        self.a.wait_recv()
        part = r.slot(self.whole, pl.ds(0, 2), place(r.s - 1), slice(None), c)
        a = self.wires.copy(part, part, r.to_s(1))
        self.b.wait_recv()
        part = r.slot(self.whole, pl.ds(2, 2), place(r.s + 1), slice(None), c)
        b = self.wires.copy(part, part, r.to_s(-1))
        self.a, self.b = a, b

    def finish(self):
        self.a.wait_recv()
        self.b.wait_recv()


def added(*terms):
    total = terms[0].astype(jnp.float32)
    for term in terms[1:]:
        total = total + term.astype(jnp.float32)
    return total


class Scatter:
    def __init__(self, ring, wires, grads, bufs, final, z, start, width, offset, far):
        self.ring, self.wires, self.grads, self.final, self.z = ring, wires, grads, final, z
        self.r1, self.r2, self.sums, self.r3, self.r4 = bufs
        self.cols = pl.ds(start, width)
        self.near = pl.ds(offset, width)
        self.far, self.start = far, start

    def one(self):
        r, c, n = self.ring, self.cols, self.near
        far = place(r.s + 2)
        self.a = self.wires.copy(
            r.slot(self.grads, pl.ds(0, 2), far, slice(None), c), self.r1.at[0, :, :, n], r.to_s(1)
        )
        self.b = self.wires.copy(
            r.slot(self.grads, pl.ds(2, 2), far, slice(None), c), self.r1.at[1, :, :, n], r.to_s(-1)
        )

    def two(self):
        r, c, n = self.ring, self.cols, self.near
        after, before = place(r.s + 1), place(r.s - 1)
        self.a.wait_recv()
        for i in range(2):
            at = r.index(i, after) + (slice(None), c)
            self.grads[at] = added(self.grads[at], self.r1[0, i, :, n]).astype(jnp.bfloat16)
        a = self.wires.copy(
            r.slot(self.grads, slice(None), after, slice(None), c), self.r2.at[0, :, :, n], r.to_s(1)
        )
        self.b.wait_recv()
        for i in range(2):
            at = r.index(2 + i, before) + (slice(None), c)
            self.grads[at] = added(self.grads[at], self.r1[1, i, :, n]).astype(jnp.bfloat16)
        b = self.wires.copy(
            r.slot(self.grads, slice(None), before, slice(None), c),
            self.r2.at[1, :, :, n],
            r.to_s(-1),
        )
        self.a, self.b = a, b

    def three(self):
        r, c, n = self.ring, self.cols, self.near
        self.a.wait_recv()
        self.b.wait_recv()
        for i in range(4):
            at = r.index(i, r.s) + (slice(None), c)
            self.sums[i, :, n] = added(
                self.grads[at], self.r2[0, i, :, n], self.r2[1, i, :, n]
            ).astype(jnp.bfloat16)
        far = place(r.f + 2)
        self.a = self.wires.copy(
            self.sums.at[far, pl.ds(0, CUT), n], self.r3.at[pl.ds(0, CUT), n], r.to_f(1)
        )
        self.b = self.wires.copy(
            self.sums.at[far, pl.ds(CUT, 80 - CUT), n],
            self.r3.at[pl.ds(CUT, 80 - CUT), n],
            r.to_f(-1),
        )

    def four(self):
        r, n = self.ring, self.near
        after, before = place(r.f + 1), place(r.f - 1)
        top, low = pl.ds(0, CUT), pl.ds(CUT, 80 - CUT)
        self.a.wait_recv()
        self.sums[after, top, n] = added(self.sums[after, top, n], self.r3[top, n]).astype(
            jnp.bfloat16
        )
        a = self.wires.copy(self.sums.at[after, :, n], self.r4.at[0, :, n], r.to_f(1))
        self.b.wait_recv()
        self.sums[before, low, n] = added(self.sums[before, low, n], self.r3[low, n]).astype(
            jnp.bfloat16
        )
        b = self.wires.copy(self.sums.at[before, :, n], self.r4.at[1, :, n], r.to_f(-1))
        self.a, self.b = a, b

    def five(self):
        r, c, n = self.ring, self.cols, self.near
        self.a.wait_recv()
        self.b.wait_recv()
        self.final[self.z, :, c] = added(
            self.sums[r.f, :, n], self.r4[0, :, n], self.r4[1, :, n]
        ).astype(jnp.bfloat16)
        part = self.final.at[self.z, :, c]
        self.zs = [self.wires.copy(part, part, {"ctx": place(self.z + k)}) for k in (1, 3, 2)]
        if self.far is not None:
            part = self.final.at[self.z, :, pl.ds(self.start, 128)]
            self.zs += [self.wires.copy(part, self.far[0], target) for target in self.far[1]]

    def finish(self):
        for made in self.zs:
            made.wait_recv()


def spot():
    d = lax.axis_index("dp")
    return lax.rem(d, 4), lax.div(d, 4), lax.axis_index("ctx")


def dot(a, b, dims=NN):
    return lax.dot_general(a, b, (dims, ((), ())), preferred_element_type=F32)


def rms(field):
    return lax.rsqrt(jnp.mean(field * field, axis=-1, keepdims=True) + EPSILON)


def norm_back(field, gain, grad):
    r = rms(field)
    hat = field * r
    scaled = grad * gain
    back = r * (scaled - hat * jnp.mean(scaled * hat, axis=-1, keepdims=True))
    return back, jnp.sum(grad * hat, axis=0, keepdims=True)


def turn(field, cos, sin):
    a, b = field[:, :128], field[:, 128:]
    return jnp.concatenate([a * cos - b * sin, b * cos + a * sin], axis=1)


def turn_back(field, cos, sin):
    a, b = field[:, :128], field[:, 128:]
    return jnp.concatenate([a * cos + b * sin, b * cos - a * sin], axis=1)


def fold(block):
    half = block.shape[-1] // 2
    return jnp.concatenate([block[..., :half], block[..., half:]], axis=-2)


def unfold(block):
    rows = block.shape[-2] // 2
    return jnp.concatenate([block[..., :rows, :], block[..., rows:, :]], axis=-1)


def iota(shape, axis):
    return lax.broadcasted_iota(jnp.int32, shape, axis)


SCRATCH = dict(
    wire=((80, WIRE), LOW),
    whole=((4, 4, 80, WIRE), LOW),
    tall=((128, 256), F32),
    wq=((D, 512), LOW),
    wkv=((D, HD), LOW),
    wo=((D, 512), LOW),
    wg=((D, FFH), LOW),
    wu=((D, FFH), LOW),
    wd=((D, FFH), LOW),
    gains=((8, D), F32),
    heads=((8, HD), F32),
    dgains=((8, D), F32),
    ends=((16, 16, 128), F32),
    end_snd=((4, 4, 16, 128), LOW),
    end_rcv=((4, 4, 16, 128), LOW),
    end_mid=((4, 16, 128), LOW),
    end_mrc=((4, 16, 128), LOW),
    end_z=((4, 16, 128), LOW),
    end_far=((4, 16, 128), LOW),
    dheads=((8, HD), F32),
    tokh=((ROWS, D), LOW),
    segp=((1, ROWS), jnp.int32),
    lo_col=((ROWS, 128), F32),
    lo_row=((8, ROWS), F32),
    cos=((1024, 128), F32),
    sin=((1024, 128), F32),
    n1=((1024, D), LOW),
    n1t=((D, 1024), LOW),
    kvb=((2, 1024, HD), LOW),
    kvraw=((1024, HD), F32),
    qraw=((4, 256, HD), F32),
    q=((4, 256, HD), LOW),
    o=((ROWS, 512), LOW),
    go=((4, 256, HD), LOW),
    gqr=((ROWS, 512), LOW),
    a=((ROWS, D), F32),
    h=((ROWS, D), F32),
    n2=((ROWS, D), LOW),
    n2t=((D, ROWS), LOW),
    ga=((ROWS, FFH), F32),
    gb=((ROWS, FFH), F32),
    u=((ROWS, FFH), LOW),
    ggu=((ROWS, 2 * FFH), LOW),
    gf=((ROWS, D), LOW),
    gft=((D, ROWS), LOW),
    gal=((ROWS, D), LOW),
    gat=((D, ROWS), LOW),
    gh=((ROWS, D), F32),
    snd=((2, ROWS, D), LOW),
    rcv=((2, ROWS, D), LOW),
    gkv=((2, 1024, HD), F32),
    kvs=((1024, HD), LOW),
    kvr=((1024, HD), LOW),
    hs=((ROWS, HD), LOW),
    hr=((ROWS, HD), LOW),
    gkr=((1024, HD), LOW),
    gko=((ROWS, HD), LOW),
    final=((4, 80, WIRE), LOW),
    far=((4, 80, 128), LOW),
)


ORDER = (
    "w0", "w1", "p1.one", "p0.one", "w2", "p2.one", "tab", "w3", "p1.two", "p3.one", "p0.three",
    "p2.two", "p1.three", "p3.two", "p0.four", "p2.three", "p1.four", "p3.three", "c0", "c1",
    "mask", "c2", "A0", "A1", "p2.four", "c3", "A2", "A3", "h0", "c4", "p3.four", "h1", "c6",
    "F0", "c8", "F1", "c9", "o0", "FB0", "G0", "o1", "FB1", "PA", "sa.one", "G1", "PB",
    "sb.one", "N0", "B0", "sa.two", "P3", "s3.one", "sb.two", "N1", "P1", "s1.one", "B1",
    "sa.three", "s3.two", "B2", "B3", "sb.three", "sa.four", "PQ", "V0", "V1", "KB", "s0.one",
    "sb.four", "s1.two", "s3.three", "QS", "NN0", "s0.two", "sb.five", "NN1", "sa.five",
    "s1.three", "s3.four", "I0", "I1", "EX", "se.one", "s0.three", "sb.fin", "s1.four",
    "s3.five", "se.two", "s0.four", "sa.fin", "s1.five", "se.five", "s0.five", "s3.fin",
    "s1.fin", "se.fin", "s0.fin",
)


def layer_kernel(tok, seg_row, cot, wq, wkv, wo, wgu, wd, ng, hg, out, igrad, grads, ends, *rest):
    names = list(SCRATCH)
    g = types.SimpleNamespace(**dict(zip(names, rest[: len(names)])))
    rest = rest[len(names) :]
    bufs = (rest[0:5], rest[5:10])
    x, y, z = spot()
    core = lax.axis_index("tensor")
    mate = {"tensor": 1 - core}
    rings = (Ring("x", x, y), Ring("y", x, y))
    gather_wires = Wires(rest[10], rest[11])
    scatter_wires = Wires(rest[12], rest[13])
    other = Wires(rest[14], rest[15])
    along_z = [{"ctx": place(z + k)} for k in (1, 3, 2)]
    across = [{"ctx": place(z + k), "tensor": 1 - core} for k in range(4)]
    targets = [r.to_f(k) for r in rings for k in (1, -1, 2)] + along_z + across
    barrier = pltpu.get_barrier_semaphore()
    for target in targets:
        pl.semaphore_signal(barrier, inc=1, device_id=target, device_id_type=MESH)

    jobs, held = {}, {}

    def job(name):
        def keep(work):
            jobs[name] = work
            return work

        return keep

    def steps(name, members, methods):
        for method in methods:
            jobs[name + "." + method] = lambda method=method: [getattr(m, method)() for m in members]

    for number, piece in enumerate(GATHERS):
        steps(
            "p%d" % number,
            [
                Gather(ring, gather_wires, g.wire, g.whole, number == 0, *piece[i])
                for i, ring in enumerate(rings)
            ],
            ("one", "two", "three", "four", "finish"),
        )
    offsets = [0, 0]
    for name, *piece in SCATTERS:
        made = []
        for i, ring in enumerate(rings):
            start, width = piece[i]
            far = (g.far.at[z], across) if start == KV else None
            made.append(
                Scatter(ring, scatter_wires, g.whole, bufs[i], g.final, z, start, width, offsets[i], far)
            )
            offsets[i] += width
        steps(name, made, ("one", "two", "three", "four", "five", "finish"))

    halves = [slice(0, 256), slice(256, 512)]

    def swap(name, number, rows, value):
        g.snd[number, rows] = value.astype(LOW)
        held[name] = other.copy(g.snd.at[number, rows], g.rcv.at[number, rows], mate)

    def total(name, number, rows):
        held[name].wait_recv()
        held[name].wait_send()
        return g.snd[number, rows].astype(F32) + g.rcv[number, rows].astype(F32)

    @job("w0")
    def _():
        g.tall[...] = jnp.zeros((128, 256), F32)
        mine = wkv[:, pl.ds(pl.multiple_of(core * HD, HD), HD)]
        g.wire[:, KV:QUERY] = fold(mine.astype(F32)).astype(LOW)
        g.wire[:, QUERY:EXTRA] = fold(wq[...].astype(F32)).astype(LOW)
        g.tall[0:4, 0:40] = ng[...].astype(F32)
        g.tall[0:2, 128:144] = hg[...].astype(F32)
        first = jnp.transpose(g.tall[:, 0:128])[:40]
        second = jnp.transpose(g.tall[:, 128:256])[:40]
        g.wire[:, EXTRA:OUT] = jnp.concatenate([first, second], axis=0).astype(LOW)
        g.whole[y, x, :, KV:OUT] = g.wire[:, KV:OUT]
        pl.semaphore_wait(barrier, len(targets))

    @job("w1")
    def _():
        held["seg"] = other.copy(seg_row, g.segp, {"ctx": place(z + 1)})
        held["tok"] = other.copy(tok, g.tokh, {"ctx": place(z + 1)})
        g.wire[:, OUT:GATEUP] = fold(wo[...].astype(F32)).astype(LOW)
        g.whole[y, x, :, OUT:GATEUP] = g.wire[:, OUT:GATEUP]

    @job("w2")
    def _():
        both = jnp.concatenate([wgu[0].astype(F32), wgu[1].astype(F32)], axis=0)
        g.wire[:, GATEUP:DOWN] = both.astype(LOW)
        g.whole[y, x, :, GATEUP:DOWN] = g.wire[:, GATEUP:DOWN]

    @job("w3")
    def _():
        g.wire[:, DOWN:WIRE] = fold(wd[...].astype(F32)).astype(LOW)
        g.whole[y, x, :, DOWN:WIRE] = g.wire[:, DOWN:WIRE]

    @job("tab")
    def _():
        rates = jnp.exp(iota((1, 128), 1).astype(F32) * (-2.0 * math.log(10000.0) / HD))
        fine = iota((128, 128), 0).astype(F32) * rates
        fine_cos, fine_sin = jnp.cos(fine), jnp.sin(fine)
        coarse = (iota((8, 128), 0) * 128 + (z * ROWS - ROWS)).astype(F32) * rates
        coarse_cos, coarse_sin = jnp.cos(coarse), jnp.sin(coarse)
        for i in range(8):
            cc, cs = coarse_cos[i : i + 1], coarse_sin[i : i + 1]
            g.cos[128 * i : 128 * i + 128] = fine_cos * cc - fine_sin * cs
            g.sin[128 * i : 128 * i + 128] = fine_sin * cc + fine_cos * cs
        g.dgains[...] = jnp.zeros((8, D), F32)
        g.dheads[...] = jnp.zeros((8, HD), F32)
        g.gkv[...] = jnp.zeros((2, 1024, HD), F32)
        g.ends[...] = jnp.zeros((16, 16, 128), F32)

    @job("mask")
    def _():
        held["seg"].wait_recv()
        own_ids, prior_ids = seg_row[...].astype(F32), g.segp[...].astype(F32)
        column = jnp.transpose(jnp.broadcast_to(own_ids, (128, ROWS)))[:, 0:1]
        below_prior = jnp.sum((prior_ids < column).astype(F32), axis=1, keepdims=True)
        below_prior = jnp.where(z == 0, float(ROWS), below_prior)
        below_own = jnp.sum((own_ids < column).astype(F32), axis=1, keepdims=True)
        lowest = jnp.maximum(below_prior + below_own, iota((ROWS, 1), 0).astype(F32) + 1.0)
        lowest = jnp.broadcast_to(lowest, (ROWS, 128))
        g.lo_col[...] = lowest
        g.lo_row[...] = jnp.transpose(lowest)[0:8]

    def assemble(first, second, start, width, w=128):
        def one(i, carry):
            at = pl.multiple_of(i * w, w)
            block = g.whole[:, :, :, pl.ds(start + at, w)].astype(F32)
            first[:, pl.ds(at, w)] = block[:, :, :40].reshape(D, w).astype(LOW)
            if second is None:
                first[:, pl.ds(at + width, w)] = block[:, :, 40:].reshape(D, w).astype(LOW)
            else:
                second[:, pl.ds(at, w)] = block[:, :, 40:].reshape(D, w).astype(LOW)
            return carry

        lax.fori_loop(0, width // w, one, 0)

    def gain(i):
        return g.gains[i : i + 1]

    def keys_of(start, normed):
        at = slice(start, start + 256)
        low = normed.astype(LOW)
        g.n1[at] = low
        raw = dot(low, g.wkv[...])
        g.kvraw[at] = raw
        turned = turn(raw * rms(raw) * g.heads[1:2], g.cos[at], g.sin[at])
        g.kvb[core, at] = jnp.where(core == 0, turned, raw).astype(LOW)
        g.n1t[:, at] = jnp.transpose(normed).astype(LOW)

    @job("c0")
    def _():
        jobs["p0.finish"]()
        block = g.whole[:, :, :, EXTRA:OUT].astype(F32)
        g.gains[...] = jnp.transpose(block[:, :, :40].reshape(D, 128))[:8]
        spread = jnp.transpose(block[:, :, 40:].reshape(D, 128))[:8]
        column_at, head_at = iota((D, HD), 0), iota((D, HD), 1)
        pick = (column_at == 40 * (head_at >> 4) + (head_at & 15)).astype(F32).astype(LOW)
        g.heads[...] = dot(spread.astype(LOW), pick)
        assemble(g.wkv, None, KV, 128)
        for rows in halves:
            block = tok[rows].astype(F32)
            keys_of(ROWS + rows.start, block * rms(block) * gain(0))
        part = g.kvb.at[core, pl.ds(ROWS, ROWS)]
        held["kv1"] = other.copy(part, part, mate)

    @job("c1")
    def _():
        held["tok"].wait_recv()
        for rows in halves:
            block = g.tokh[rows].astype(F32)
            keys_of(rows.start, block * rms(block) * gain(0))
        part = g.kvb.at[core, pl.ds(0, ROWS)]
        held["kv2"] = other.copy(part, part, mate)

    @job("c2")
    def _():
        assemble(g.wq, None, QUERY, 256)
        for i in range(2):
            at = slice(ROWS + 256 * i, ROWS + 256 * i + 256)
            raw = dot(g.n1[at], g.wq[...])
            for h in range(2):
                part = raw[:, HD * h : HD * h + HD]
                turned = turn(part * rms(part) * g.heads[0:1], g.cos[at], g.sin[at]).astype(LOW)
                for j in range(2):
                    g.qraw[2 * i + j, 128 * h : 128 * h + 128] = part[128 * j : 128 * j + 128]
                    g.q[2 * i + j, 128 * h : 128 * h + 128] = turned[128 * j : 128 * j + 128]

    def twice(block, axis):
        return jnp.concatenate([block, block], axis=axis)

    def attend(b, carry):
        start = pl.multiple_of(b * 128, 128)
        keys, values = g.kvb[0, pl.ds(start, D)], g.kvb[1, pl.ds(start, D)]
        scores = dot(g.q[b], keys, NT) * SCALE
        lowest = twice(g.lo_col[pl.ds(start, 128), 0:1], 0) - (b * 128).astype(F32)
        place_k = iota((256, D), 1).astype(F32)
        highest = (iota((256, 1), 0) & 127).astype(F32) + float(WINDOW)
        scores = jnp.where((place_k >= lowest) & (place_k <= highest), scores, -1e30)
        expo = jnp.exp(scores - jnp.max(scores, axis=-1, keepdims=True))
        probs = (expo / jnp.sum(expo, axis=-1, keepdims=True)).astype(LOW)
        mixed = dot(probs, values).astype(LOW)
        g.o[pl.ds(start, 128), 0:HD] = mixed[:128]
        g.o[pl.ds(start, 128), HD : 2 * HD] = mixed[128:]
        return carry

    @job("A0")
    def _():
        held["kv1"].wait_recv()
        held["kv2"].wait_recv()
        lax.fori_loop(0, 1, attend, 0)

    for b in (1, 2, 3):
        jobs["A%d" % b] = lambda b=b: lax.fori_loop(b, b + 1, attend, 0)

    @job("c3")
    def _():
        jobs["p1.finish"]()
        assemble(g.wo, None, OUT, 256)
        swap("a0", 0, halves[0], dot(g.o[halves[0]], g.wo[...], NT))

    @job("c4")
    def _():
        swap("a1", 0, halves[1], dot(g.o[halves[1]], g.wo[...], NT))

    def hidden_rows(i):
        rows = halves[i]
        branch = total("a%d" % i, 0, rows)
        g.a[rows] = branch
        hidden = tok[rows].astype(F32) + branch * rms(branch) * gain(1)
        g.h[rows] = hidden
        normed = hidden * rms(hidden) * gain(2)
        g.n2[rows] = normed.astype(LOW)
        g.n2t[:, rows] = jnp.transpose(normed).astype(LOW)

    c0, c1 = math.sqrt(2.0 / math.pi), 0.044715

    def forward_rows(k):
        rows = halves[k]

        def one(i, carry):
            cols = pl.ds(pl.multiple_of(i * 256, 256), 256)
            gate = dot(g.n2[rows], g.wg[:, cols])
            up = dot(g.n2[rows], g.wu[:, cols])
            square = gate * gate
            t = jnp.tanh(c0 * gate * (1.0 + c1 * square))
            act = 0.5 * gate * (1.0 + t)
            slope = 0.5 * (1.0 + t) + 0.5 * gate * (1.0 - t * t) * (c0 * (1.0 + 3.0 * c1 * square))
            g.ga[rows, cols] = act
            g.gb[rows, cols] = up * slope
            g.u[rows, cols] = (act * up).astype(LOW)
            return carry

        lax.fori_loop(0, 4, one, 0)

    @job("c6")
    def _():
        jobs["p2.finish"]()
        assemble(g.wg, g.wu, GATEUP, FFH)

    @job("c8")
    def _():
        jobs["p3.finish"]()
        gather_wires.drain()
        assemble(g.wd, None, DOWN, 512)
        swap("f0", 1, halves[0], dot(g.u[halves[0]], g.wd[...], NT))

    @job("c9")
    def _():
        swap("f1", 1, halves[1], dot(g.u[halves[1]], g.wd[...], NT))

    def output_rows(i):
        rows = halves[i]
        feed = total("f%d" % i, 1, rows)
        out[rows] = (g.h[rows] + feed * rms(feed) * gain(3)).astype(LOW)
        back, slope = norm_back(feed, gain(3), cot[rows].astype(F32))
        g.dgains[3:4] += slope
        g.gf[rows] = back.astype(LOW)
        g.gft[:, rows] = jnp.transpose(back).astype(LOW)

    def put(left, right, start, begin, end, gap, w=256):
        def one(i, carry):
            at = pl.multiple_of(i * w, w)
            first = dot(left[...], right[:, pl.ds(at, w)]).reshape(16, 40, w)
            second = dot(left[...], right[:, pl.ds(at + gap, w)]).reshape(16, 40, w)
            block = jnp.concatenate([first, second], axis=1).astype(LOW)
            g.whole[:, :, :, pl.ds(start + at, w)] = block.reshape(4, 4, 80, w)
            return carry

        lax.fori_loop(begin // w, end // w, one, 0)

    jobs["P3"] = lambda: put(g.gft, g.u, DOWN, 0, 512, 512)
    jobs["PA"] = lambda: put(g.n2t, g.ggu, GATEUP, 0, 512, FFH)
    jobs["PB"] = lambda: put(g.n2t, g.ggu, GATEUP, 512, 1024, FFH)
    jobs["P1"] = lambda: put(g.gat, g.o, OUT, 0, 256, 256)
    jobs["PQ"] = lambda: put(g.n1t.at[:, ROWS:], g.gqr, QUERY, 0, 256, 256)

    def backward_rows(k):
        rows = halves[k]

        def one(i, carry):
            at = pl.multiple_of(i * 256, 256)
            cols = pl.ds(at, 256)
            inner = dot(g.gf[rows], g.wd[:, cols])
            g.ggu[rows, cols] = (inner * g.gb[rows, cols]).astype(LOW)
            g.ggu[rows, pl.ds(at + FFH, 256)] = (inner * g.ga[rows, cols]).astype(LOW)
            return carry

        lax.fori_loop(0, 4, one, 0)

    def second_rows(i):
        rows = halves[i]
        part = dot(g.ggu[rows, 0:FFH], g.wg[...], NT) + dot(g.ggu[rows, FFH:], g.wu[...], NT)
        swap("g%d" % i, 0, rows, part)

    def norm_rows(i):
        rows = halves[i]
        back, slope = norm_back(g.h[rows], gain(2), total("g%d" % i, 0, rows))
        g.dgains[2:3] += slope
        hidden = cot[rows].astype(F32) + back
        g.gh[rows] = hidden
        back, slope = norm_back(g.a[rows], gain(1), hidden)
        g.dgains[1:2] += slope
        g.gat[:, rows] = jnp.transpose(back).astype(LOW)
        grad = dot(back.astype(LOW), g.wo[...]).astype(LOW)
        for j in range(2):
            for h in range(2):
                g.go[2 * i + j, 128 * h : 128 * h + 128] = grad[
                    128 * j : 128 * j + 128, HD * h : HD * h + HD
                ]

    for i in range(2):
        jobs["h%d" % i] = lambda i=i: hidden_rows(i)
        jobs["F%d" % i] = lambda i=i: forward_rows(i)
        jobs["o%d" % i] = lambda i=i: output_rows(i)
        jobs["FB%d" % i] = lambda i=i: backward_rows(i)
        jobs["G%d" % i] = lambda i=i: second_rows(i)
        jobs["N%d" % i] = lambda i=i: norm_rows(i)

    def attend_back(b, carry):
        start = pl.multiple_of(b * 128, 128)
        keys, values = g.kvb[0, pl.ds(start, D)], g.kvb[1, pl.ds(start, D)]
        queries, grad = g.q[b], g.go[b]
        scores = dot(keys, queries, NT) * SCALE
        lowest = twice(g.lo_row[0:1, pl.ds(start, 128)], 1) - (b * 128).astype(F32)
        place_k = iota((D, 256), 0).astype(F32)
        highest = (iota((1, 256), 1) & 127).astype(F32) + float(WINDOW)
        scores = jnp.where((place_k >= lowest) & (place_k <= highest), scores, -1e30)
        expo = jnp.exp(scores - jnp.max(scores, axis=0, keepdims=True))
        probs = expo * (1.0 / jnp.sum(expo, axis=0, keepdims=True))
        grad_probs = dot(values, grad, NT)
        spread = jnp.sum(probs * grad_probs, axis=0, keepdims=True)
        grad_scores = (probs * (grad_probs - spread)).astype(LOW)
        g.gkv[0, pl.ds(start, D)] += dot(grad_scores, queries) * SCALE
        g.gkv[1, pl.ds(start, D)] += dot(probs.astype(LOW), grad)
        grad_q = dot(grad_scores, keys, TN) * SCALE
        at = pl.ds(pl.multiple_of(ROWS + start, 128), 128)
        grad_q = turn_back(grad_q, twice(g.cos[at], 0), twice(g.sin[at], 0))
        back, slope = norm_back(g.qraw[b], g.heads[0:1], grad_q)
        g.dheads[0:1] += slope
        g.gqr[pl.ds(start, 128), 0:HD] = back[:128].astype(LOW)
        g.gqr[pl.ds(start, 128), HD : 2 * HD] = back[128:].astype(LOW)
        return carry

    def back_block(b):
        lax.fori_loop(b, b + 1, attend_back, 0)
        if b in (1, 3):
            rows = pl.ds(0, 256) if b == 1 else pl.ds(256, 768)
            g.kvs[rows] = g.gkv[1 - core, rows].astype(LOW)
            held["kvx%d" % (b // 2)] = other.copy(g.kvs.at[rows], g.kvr.at[rows], mate)

    for b in range(4):
        jobs["B%d" % b] = lambda b=b: back_block(b)

    def summed_rows(i):
        rows = slice(0, 256) if i == 0 else slice(256, 1024)
        held["kvx%d" % i].wait_recv()
        g.gkv[core, rows] = added(g.gkv[core, rows], g.kvr[rows])
        g.hs[halves[i]] = g.gkv[core, halves[i]].astype(LOW)
        held["ha%d" % i] = other.copy(
            g.hs.at[halves[i]], g.hr.at[halves[i]], {"ctx": place(z - 1)}
        )

    def keys_back(start, grad):
        at = slice(start, start + 256)
        turned = turn_back(grad, g.cos[at], g.sin[at])
        back, slope = norm_back(g.kvraw[at], g.heads[1:2], turned)
        return jnp.where(core == 0, back, grad).astype(LOW), jnp.where(core == 0, slope, 0.0)

    @job("KB")
    def _():
        for start in range(0, 1024, 256):
            low, slope = keys_back(start, g.gkv[core, start : start + 256])
            g.dheads[1:2] += slope
            g.gkr[start : start + 256] = low
        put(g.n1t, g.gkr, KV, 0, 128, 128, w=128)

    @job("QS")
    def _():
        for rows in halves:
            g.a[rows] = dot(g.gqr[rows], g.wq[...], NT)

    def first_rows(i):
        rows = halves[i]
        held["ha%d" % i].wait_recv()
        start = ROWS + rows.start
        grad = added(g.gkv[core, start : start + 256], g.hr[rows])
        low, _ = keys_back(start, grad)
        swap("n%d" % i, 1, rows, g.a[rows] + dot(low, g.wkv[...], NT))

    def input_rows(i):
        rows = halves[i]
        back, slope = norm_back(tok[rows].astype(F32), gain(0), total("n%d" % i, 1, rows))
        g.dgains[0:1] += slope
        igrad[rows] = g.gh[rows] + back

    for i in range(2):
        jobs["V%d" % i] = lambda i=i: summed_rows(i)
        jobs["NN%d" % i] = lambda i=i: first_rows(i)
        jobs["I%d" % i] = lambda i=i: input_rows(i)

    @job("EX")
    def _():
        for d in range(16):
            g.ends[d, 0:8, 0:40] = g.dgains[:, 40 * d : 40 * d + 40]
            g.ends[d, 8:16, 0:16] = g.dheads[:, 16 * d : 16 * d + 16]
        g.end_snd[...] = g.ends[...].astype(LOW).reshape(4, 4, 16, 128)

    @job("se.one")
    def _():
        held["se"] = [
            other.copy(g.end_snd.at[place(y + k)], g.end_rcv.at[y], {"dp": place(y + k) * 4 + x})
            for k in (1, 3, 2)
        ]

    @job("se.two")
    def _():
        for made in held["se"]:
            made.wait_recv()
        g.end_rcv[y] = g.end_snd[y]
        g.end_mid[...] = added(*(g.end_rcv[i] for i in range(4))).astype(LOW)
        held["se"] = [
            other.copy(g.end_mid.at[place(x + k)], g.end_mrc.at[x], {"dp": y * 4 + place(x + k)})
            for k in (1, 3, 2)
        ]

    @job("se.five")
    def _():
        for made in held["se"]:
            made.wait_recv()
        g.end_mrc[x] = g.end_mid[x]
        g.end_z[z] = added(*(g.end_mrc[i] for i in range(4))).astype(LOW)
        held["se"] = [other.copy(g.end_z.at[z], g.end_z.at[z], target) for target in along_z] + [
            other.copy(g.end_z.at[z], g.end_far.at[z], target) for target in across
        ]

    @job("se.fin")
    def _():
        for made in held["se"]:
            made.wait_recv()
        own = added(*(g.end_z[i] for i in range(4)))
        far = added(*(g.end_far[i] for i in range(4)))
        ends[0:8] = own[0:8]
        ends[8:16] = own[8:16] + far[8:16]

    def put_final(name, source, start, at, width):
        def work():
            jobs[name + ".finish"]()
            cols = pl.ds(start, width)
            grads[:, at : at + width] = added(*(source[i, :, cols] for i in range(4)))

        jobs[name + ".fin"] = work

    put_final("s3", g.final, DOWN, DOWN, 512)
    put_final("sa", g.final, GATEUP, GATEUP, 512)
    put_final("sb", g.final, GATEUP + 512, GATEUP + 512, 512)
    put_final("s1", g.final, OUT, OUT, 256)

    @job("s0.fin")
    def _():
        jobs["s0.finish"]()
        own = added(*(g.final[i, :, KV:QUERY] for i in range(4)))
        far = added(*(g.far[i] for i in range(4)))
        grads[:, 0:128] = jnp.where(core == 0, own, far)
        grads[:, EXTRA:OUT] = jnp.where(core == 0, far, own)
        grads[:, QUERY:EXTRA] = added(*(g.final[i, :, QUERY:EXTRA] for i in range(4)))

    for name in ORDER:
        jobs[name]()
    scatter_wires.drain()
    waited = [held[n + str(i)] for n in "afgn" for i in (0, 1)]
    for made in other.started:
        if not any(made is one for one in waited):
            made.wait_send()


def hand_out(output, input_grad, done, ends, out, igrad, query, keyval, wide, gateup, down, norms, heads, sems):
    copies = [
        pltpu.make_async_copy(output, out, sems.at[0]),
        pltpu.make_async_copy(input_grad, igrad, sems.at[1]),
    ]
    for made in copies:
        made.start()
    keyval[:, 0:256] = unfold(done[:, KV:QUERY])
    keyval[:, 256:512] = unfold(done[:, EXTRA:OUT])
    query[...] = unfold(done[:, QUERY:EXTRA])
    wide[...] = unfold(done[:, OUT:GATEUP])
    gateup[0] = done[:40, GATEUP:DOWN]
    gateup[1] = done[40:, GATEUP:DOWN]
    down[...] = unfold(done[:, DOWN:WIRE])
    norms[...] = ends[0:4, 0:40]
    heads[...] = ends[8:10, 0:16]
    for made in copies:
        made.wait()


def vmem():
    return pl.BlockSpec(memory_space=pltpu.VMEM)


def ring_buffers(cols):
    return [
        pltpu.VMEM((2, 2, 80, cols), LOW),
        pltpu.VMEM((2, 4, 80, cols), LOW),
        pltpu.VMEM((4, 80, cols), LOW),
        pltpu.VMEM((80, cols), LOW),
        pltpu.VMEM((2, 80, cols), LOW),
    ]


def shards(
    tokens, segments, cotangent, w_query, w_keyval, w_out, w_gateup, w_down, norm_gains, head_gains
):
    output, input_grad, done, ends = pl.pallas_call(
        layer_kernel,
        out_shape=(
            jax.ShapeDtypeStruct((ROWS, D), LOW),
            jax.ShapeDtypeStruct((ROWS, D), F32),
            jax.ShapeDtypeStruct((80, WIRE), F32),
            jax.ShapeDtypeStruct((16, 128), F32),
        ),
        in_specs=[vmem()] * 10,
        out_specs=(vmem(),) * 4,
        scratch_shapes=[
            *(pltpu.VMEM(*shape) for shape in SCRATCH.values()),
            *ring_buffers(SET_COLS[0]),
            *ring_buffers(SET_COLS[1]),
            pltpu.SemaphoreType.DMA((64,)),
            pltpu.SemaphoreType.DMA((64,)),
            pltpu.SemaphoreType.DMA((128,)),
            pltpu.SemaphoreType.DMA((128,)),
            pltpu.SemaphoreType.DMA((40,)),
            pltpu.SemaphoreType.DMA((40,)),
        ],
        compiler_params=pltpu.CompilerParams(
            collective_id=0, has_side_effects=True, vmem_limit_bytes=VMEM_BYTES
        ),
    )(
        tokens[0],
        segments,
        cotangent[0],
        w_query,
        w_keyval,
        w_out.T,
        w_gateup,
        w_down.T,
        norm_gains,
        head_gains,
    )
    whole = pl.BlockSpec(memory_space=pl.ANY)
    results = pl.pallas_call(
        hand_out,
        out_shape=(
            jax.ShapeDtypeStruct((ROWS, D), LOW),
            jax.ShapeDtypeStruct((ROWS, D), F32),
            jax.ShapeDtypeStruct((40, 512), F32),
            jax.ShapeDtypeStruct((40, 512), F32),
            jax.ShapeDtypeStruct((40, 512), F32),
            jax.ShapeDtypeStruct((2, 40, FFH), F32),
            jax.ShapeDtypeStruct((40, FFH), F32),
            jax.ShapeDtypeStruct((4, 40), F32),
            jax.ShapeDtypeStruct((2, 16), F32),
        ),
        in_specs=[whole, whole, vmem(), vmem()],
        out_specs=(whole, whole) + (vmem(),) * 7,
        scratch_shapes=[pltpu.SemaphoreType.DMA((2,))],
        compiler_params=pltpu.CompilerParams(vmem_limit_bytes=VMEM_BYTES),
    )(output, input_grad, done, ends)
    return (
        results[0][None],
        results[1][None],
        results[2],
        results[3],
        results[4].T,
        results[5],
        results[6].T,
        results[7],
        results[8],
    )


def solution(mesh):
    placed = (
        P("dp", "ctx", None),
        P("dp", "ctx"),
        P("dp", "ctx", None),
        P("dp", "tensor"),
        P("dp", None),
        P("tensor", "dp"),
        P(None, "dp", "tensor"),
        P("tensor", "dp"),
        P(None, "dp"),
        P(None, "dp"),
    )
    return jax.shard_map(
        shards,
        mesh=mesh,
        in_specs=placed,
        out_specs=(
            P("dp", "ctx", None),
            P("dp", "ctx", None),
            P("dp", "tensor"),
            P("dp", None),
            P("tensor", "dp"),
            P(None, "dp", "tensor"),
            P("tensor", "dp"),
            P(None, "dp"),
            P(None, "dp"),
        ),
        check_vma=False,
    )
```

time: 122 us -> 164 us (1.34)
  Pallas kernels: 118 us -> 163 us
  local copies, waits for them, and re-layouts: 3.53 us -> 0 us
    pallas_call x1, Pallas kernels: 2.15 us -> 62.7 us  [shards(): pl.pallas_call(hand_out, out_shape=(jax.ShapeDtypeStruct((ROWS, D), LOW),...]
    pallas_call x1, Pallas kernels: 115 us -> 99.9 us  [shards(): pl.pallas_call(layer_kernel, out_shape=(jax.ShapeDtypeStruct((ROWS, D), L...]
    unnamed x6 -> x0, local copies, waits for them, and re-layouts: 3.53 us -> none
where the time goes in v2:
time: 164 us; the launch traced here: 163 us
  Pallas kernels  163 us (99%)
    pallas_call x1, Pallas kernels, shards(): pl.pallas_call(layer_kernel, out_shape=(jax.ShapeDtypeStruct((ROWS, D), L...  99.9 us
    pallas_call x1, Pallas kernels, shards(): pl.pallas_call(hand_out, out_shape=(jax.ShapeDtypeStruct((ROWS, D), LOW),...  62.7 us

profile of v2, /device:TPU:1, one launch (start us, length us, event | category | flops | bytes accessed | tf_op | source)
XLA Modules:
  0.0 163.4 jit_solution(16879698516690665254)
XLA Ops:
  0.6 99.9 %shard_map.169 = (bf16[512,640]{1,0:T(8,128)(2,1)}, f32[512,640]{1,0:T(8,128)}, f32[80,2304]{1,0:T(8,128)}, f32[16,128]{1,0:T(8,128)}) custom-call(bf16[512,640]{1,0:T(8,128)(2,1)} %bitcast.8, s32[1,512]{1,0:T(1,128)} %seg_row.1, bf16[512,640]{1,0:T(8,128)(2,1)} %bitcast.9, bf16[40,512]{1,0:T(8,128)(2,1)} %wq.1, bf16[40,512]{1,0:T(8,128)(2,1)} %wkv.1, ...), custom_call_target="tpu_custom_call" | custom-call | tf_op jit(solution)/shard_map/pallas_call | solution.py:894
  100.5 62.7 %shard_map.170 = (bf16[512,640]{1,0:T(8,128)(2,1)}, f32[512,640]{1,0:T(8,128)}, f32[40,512]{1,0:T(8,128)}, f32[40,512]{1,0:T(8,128)}, f32[40,512]{1,0:T(8,128)},...) custom-call(bf16[512,640]{1,0:T(8,128)(2,1)} %get-tuple-element.22.output, ...), custom_call_target="tpu_custom_call" | custom-call | tf_op jit(solution)/shard_map/pallas_call | solution.py:931

commit v3 on v2

--- a/solution.py
+++ b/solution.py
@@ -854,13 +854,9 @@
             made.wait_send()
 
 
-def hand_out(output, input_grad, done, ends, out, igrad, query, keyval, wide, gateup, down, norms, heads, sems):
-    copies = [
-        pltpu.make_async_copy(output, out, sems.at[0]),
-        pltpu.make_async_copy(input_grad, igrad, sems.at[1]),
-    ]
-    for made in copies:
-        made.start()
+def hand_out(output, input_grad, done, ends, out, igrad, query, keyval, wide, gateup, down, norms, heads):
+    out[...] = output[...]
+    igrad[...] = input_grad[...]
     keyval[:, 0:256] = unfold(done[:, KV:QUERY])
     keyval[:, 256:512] = unfold(done[:, EXTRA:OUT])
     query[...] = unfold(done[:, QUERY:EXTRA])
@@ -870,8 +866,6 @@
     down[...] = unfold(done[:, DOWN:WIRE])
     norms[...] = ends[0:4, 0:40]
     heads[...] = ends[8:10, 0:16]
-    for made in copies:
-        made.wait()
 
 
 def vmem():
@@ -927,7 +921,6 @@
         norm_gains,
         head_gains,
     )
-    whole = pl.BlockSpec(memory_space=pl.ANY)
     results = pl.pallas_call(
         hand_out,
         out_shape=(
@@ -941,9 +934,8 @@
             jax.ShapeDtypeStruct((4, 40), F32),
             jax.ShapeDtypeStruct((2, 16), F32),
         ),
-        in_specs=[whole, whole, vmem(), vmem()],
-        out_specs=(whole, whole) + (vmem(),) * 7,
-        scratch_shapes=[pltpu.SemaphoreType.DMA((2,))],
+        in_specs=[vmem()] * 4,
+        out_specs=(vmem(),) * 9,
         compiler_params=pltpu.CompilerParams(vmem_limit_bytes=VMEM_BYTES),
     )(output, input_grad, done, ends)
     return (

time: 164 us -> 104 us (0.63)
  Pallas kernels: 163 us -> 103 us
    pallas_call x1, Pallas kernels: 62.7 us -> 3.31 us  [shards(): pl.pallas_call(hand_out, out_shape=(jax.ShapeDtypeStruct((ROWS, D), LOW),...]
where the time goes in v3:
time: 104 us
  Pallas kernels  103 us (99%)
    pallas_call x1, Pallas kernels, shards(): pl.pallas_call(layer_kernel, out_shape=(jax.ShapeDtypeStruct((ROWS, D), L...  99.9 us
    pallas_call x1, Pallas kernels, shards(): pl.pallas_call(hand_out, out_shape=(jax.ShapeDtypeStruct((ROWS, D), LOW),...  3.31 us

profile of v3, /device:TPU:1, one launch (start us, length us, event | category | flops | bytes accessed | tf_op | source)
XLA Modules:
  0.0 103.8 jit_solution(11804647155123742502)
XLA Ops:
  0.6 99.9 %shard_map.169 = (bf16[512,640]{1,0:T(8,128)(2,1)}, f32[512,640]{1,0:T(8,128)}, f32[80,2304]{1,0:T(8,128)}, f32[16,128]{1,0:T(8,128)}) custom-call(bf16[512,640]{1,0:T(8,128)(2,1)} %bitcast.8, s32[1,512]{1,0:T(1,128)} %seg_row.1, bf16[512,640]{1,0:T(8,128)(2,1)} %bitcast.9, bf16[40,512]{1,0:T(8,128)(2,1)} %wq.1, bf16[40,512]{1,0:T(8,128)(2,1)} %wkv.1, ...), custom_call_target="tpu_custom_call" | custom-call | tf_op jit(solution)/shard_map/pallas_call | solution.py:888
  100.5 3.3 %shard_map.170 = (bf16[512,640]{1,0:T(8,128)(2,1)}, f32[512,640]{1,0:T(8,128)}, f32[40,512]{1,0:T(8,128)}, f32[40,512]{1,0:T(8,128)}, f32[40,512]{1,0:T(8,128)},...) custom-call(bf16[512,640]{1,0:T(8,128)(2,1)} %get-tuple-element.22.output, ...), custom_call_target="tpu_custom_call" | custom-call | tf_op jit(solution)/shard_map/pallas_call | solution.py:924

commit v4 on v3

--- a/solution.py
+++ b/solution.py
@@ -344,24 +344,38 @@
 
 
 ORDER = (
-    "w0", "w1", "p1.one", "p0.one", "w2", "p2.one", "tab", "w3", "p1.two", "p3.one", "p0.three",
-    "p2.two", "p1.three", "p3.two", "p0.four", "p2.three", "p1.four", "p3.three", "c0", "c1",
-    "mask", "c2", "A0", "A1", "p2.four", "c3", "A2", "A3", "h0", "c4", "p3.four", "h1", "c6",
-    "F0", "c8", "F1", "c9", "o0", "FB0", "G0", "o1", "FB1", "PA", "sa.one", "G1", "PB",
-    "sb.one", "N0", "B0", "sa.two", "P3", "s3.one", "sb.two", "N1", "P1", "s1.one", "B1",
-    "sa.three", "s3.two", "B2", "B3", "sb.three", "sa.four", "PQ", "V0", "V1", "KB", "s0.one",
-    "sb.four", "s1.two", "s3.three", "QS", "NN0", "s0.two", "sb.five", "NN1", "sa.five",
-    "s1.three", "s3.four", "I0", "I1", "EX", "se.one", "s0.three", "sb.fin", "s1.four",
-    "s3.five", "se.two", "s0.four", "sa.fin", "s1.five", "se.five", "s0.five", "s3.fin",
+    "w0", "w1", "p1.one", "p0.one", "w2", "p2.one", "tab", "mask", "p1.two", "w3", "p3.one",
+    "p0.three", "p2.two", "p1.three", "p3.two", "p0.four", "p2.three", "p1.four", "c0", "c1",
+    "p3.three", "c2", "A0", "A1", "p2.four", "c3", "A2", "A3", "c4", "h0", "p3.four", "h1",
+    "c6", "F0", "c8", "F1", "c9", "o0", "FB0", "G0", "o1", "P3", "s3.one", "FB1", "PA",
+    "sa.one", "PB", "sb.one", "G1", "N0", "s3.two", "B0", "sa.two", "B1", "sb.two", "N1", "B2",
+    "B3", "s3.three", "V0", "P1", "s1.one", "QS", "V1", "sa.three", "PQ", "KB", "s0.one",
+    "sb.three", "s3.four", "s1.two", "sa.four", "NN0", "s0.two", "sb.four", "s3.five", "NN1",
+    "I0", "s1.three", "sa.five", "I1", "EX", "se.one", "s0.three", "s3.fin", "s1.four",
+    "sb.five", "se.two", "s0.four", "sa.fin", "s1.five", "se.five", "s0.five", "sb.fin",
     "s1.fin", "se.fin", "s0.fin",
 )
 
 
-def layer_kernel(tok, seg_row, cot, wq, wkv, wo, wgu, wd, ng, hg, out, igrad, grads, ends, *rest):
+def layer_kernel(
+    tok_hbm, seg_row, cot_hbm, wq, wkv, wo, wgu, wd, ng, hg, out_hbm, igrad_hbm, grads_hbm, ends, *rest
+):
     names = list(SCRATCH)
     g = types.SimpleNamespace(**dict(zip(names, rest[: len(names)])))
     rest = rest[len(names) :]
     bufs = (rest[0:5], rest[5:10])
+    tok, cot, out, igrad, grads, local = rest[16:22]
+    tok_read = pltpu.make_async_copy(tok_hbm, tok, local.at[0])
+    cot_read = pltpu.make_async_copy(cot_hbm, cot, local.at[1])
+    tok_read.start()
+    cot_read.start()
+    writes = []
+
+    def write(source, target):
+        made = pltpu.make_async_copy(source, target, local.at[2 + len(writes)])
+        made.start()
+        writes.append(made)
+
     x, y, z = spot()
     core = lax.axis_index("tensor")
     mate = {"tensor": 1 - core}
@@ -438,6 +452,7 @@
     @job("w1")
     def _():
         held["seg"] = other.copy(seg_row, g.segp, {"ctx": place(z + 1)})
+        tok_read.wait()
         held["tok"] = other.copy(tok, g.tokh, {"ctx": place(z + 1)})
         g.wire[:, OUT:GATEUP] = fold(wo[...].astype(F32)).astype(LOW)
         g.whole[y, x, :, OUT:GATEUP] = g.wire[:, OUT:GATEUP]
@@ -483,17 +498,17 @@
         g.lo_row[...] = jnp.transpose(lowest)[0:8]
 
     def assemble(first, second, start, width, w=128):
-        def one(i, carry):
-            at = pl.multiple_of(i * w, w)
+        def one(i):
+            at = i * w
             block = g.whole[:, :, :, pl.ds(start + at, w)].astype(F32)
             first[:, pl.ds(at, w)] = block[:, :, :40].reshape(D, w).astype(LOW)
             if second is None:
                 first[:, pl.ds(at + width, w)] = block[:, :, 40:].reshape(D, w).astype(LOW)
             else:
                 second[:, pl.ds(at, w)] = block[:, :, 40:].reshape(D, w).astype(LOW)
-            return carry
-
-        lax.fori_loop(0, width // w, one, 0)
+
+        for i in range(width // w):
+            one(i)
 
     def gain(i):
         return g.gains[i : i + 1]
@@ -549,11 +564,11 @@
     def twice(block, axis):
         return jnp.concatenate([block, block], axis=axis)
 
-    def attend(b, carry):
-        start = pl.multiple_of(b * 128, 128)
+    def attend(b):
+        start = b * 128
         keys, values = g.kvb[0, pl.ds(start, D)], g.kvb[1, pl.ds(start, D)]
         scores = dot(g.q[b], keys, NT) * SCALE
-        lowest = twice(g.lo_col[pl.ds(start, 128), 0:1], 0) - (b * 128).astype(F32)
+        lowest = twice(g.lo_col[pl.ds(start, 128), 0:1], 0) - float(b * 128)
         place_k = iota((256, D), 1).astype(F32)
         highest = (iota((256, 1), 0) & 127).astype(F32) + float(WINDOW)
         scores = jnp.where((place_k >= lowest) & (place_k <= highest), scores, -1e30)
@@ -562,16 +577,15 @@
         mixed = dot(probs, values).astype(LOW)
         g.o[pl.ds(start, 128), 0:HD] = mixed[:128]
         g.o[pl.ds(start, 128), HD : 2 * HD] = mixed[128:]
-        return carry
 
     @job("A0")
     def _():
         held["kv1"].wait_recv()
         held["kv2"].wait_recv()
-        lax.fori_loop(0, 1, attend, 0)
+        attend(0)
 
     for b in (1, 2, 3):
-        jobs["A%d" % b] = lambda b=b: lax.fori_loop(b, b + 1, attend, 0)
+        jobs["A%d" % b] = lambda b=b: attend(b)
 
     @job("c3")
     def _():
@@ -598,8 +612,8 @@
     def forward_rows(k):
         rows = halves[k]
 
-        def one(i, carry):
-            cols = pl.ds(pl.multiple_of(i * 256, 256), 256)
+        def one(i):
+            cols = pl.ds(i * 256, 256)
             gate = dot(g.n2[rows], g.wg[:, cols])
             up = dot(g.n2[rows], g.wu[:, cols])
             square = gate * gate
@@ -609,9 +623,9 @@
             g.ga[rows, cols] = act
             g.gb[rows, cols] = up * slope
             g.u[rows, cols] = (act * up).astype(LOW)
-            return carry
-
-        lax.fori_loop(0, 4, one, 0)
+
+        for i in range(4):
+            one(i)
 
     @job("c6")
     def _():
@@ -631,23 +645,26 @@
 
     def output_rows(i):
         rows = halves[i]
+        if i == 0:
+            cot_read.wait()
         feed = total("f%d" % i, 1, rows)
         out[rows] = (g.h[rows] + feed * rms(feed) * gain(3)).astype(LOW)
         back, slope = norm_back(feed, gain(3), cot[rows].astype(F32))
         g.dgains[3:4] += slope
         g.gf[rows] = back.astype(LOW)
         g.gft[:, rows] = jnp.transpose(back).astype(LOW)
+        write(out.at[rows], out_hbm.at[rows])
 
     def put(left, right, start, begin, end, gap, w=256):
-        def one(i, carry):
-            at = pl.multiple_of(i * w, w)
+        def one(i):
+            at = i * w
             first = dot(left[...], right[:, pl.ds(at, w)]).reshape(16, 40, w)
             second = dot(left[...], right[:, pl.ds(at + gap, w)]).reshape(16, 40, w)
             block = jnp.concatenate([first, second], axis=1).astype(LOW)
             g.whole[:, :, :, pl.ds(start + at, w)] = block.reshape(4, 4, 80, w)
-            return carry
-
-        lax.fori_loop(begin // w, end // w, one, 0)
+
+        for i in range(begin // w, end // w):
+            one(i)
 
     jobs["P3"] = lambda: put(g.gft, g.u, DOWN, 0, 512, 512)
     jobs["PA"] = lambda: put(g.n2t, g.ggu, GATEUP, 0, 512, FFH)
@@ -658,15 +675,15 @@
     def backward_rows(k):
         rows = halves[k]
 
-        def one(i, carry):
-            at = pl.multiple_of(i * 256, 256)
+        def one(i):
+            at = i * 256
             cols = pl.ds(at, 256)
             inner = dot(g.gf[rows], g.wd[:, cols])
             g.ggu[rows, cols] = (inner * g.gb[rows, cols]).astype(LOW)
             g.ggu[rows, pl.ds(at + FFH, 256)] = (inner * g.ga[rows, cols]).astype(LOW)
-            return carry
-
-        lax.fori_loop(0, 4, one, 0)
+
+        for i in range(4):
+            one(i)
 
     def second_rows(i):
         rows = halves[i]
@@ -697,12 +714,12 @@
         jobs["G%d" % i] = lambda i=i: second_rows(i)
         jobs["N%d" % i] = lambda i=i: norm_rows(i)
 
-    def attend_back(b, carry):
-        start = pl.multiple_of(b * 128, 128)
+    def attend_back(b):
+        start = b * 128
         keys, values = g.kvb[0, pl.ds(start, D)], g.kvb[1, pl.ds(start, D)]
         queries, grad = g.q[b], g.go[b]
         scores = dot(keys, queries, NT) * SCALE
-        lowest = twice(g.lo_row[0:1, pl.ds(start, 128)], 1) - (b * 128).astype(F32)
+        lowest = twice(g.lo_row[0:1, pl.ds(start, 128)], 1) - float(b * 128)
         place_k = iota((D, 256), 0).astype(F32)
         highest = (iota((1, 256), 1) & 127).astype(F32) + float(WINDOW)
         scores = jnp.where((place_k >= lowest) & (place_k <= highest), scores, -1e30)
@@ -714,16 +731,15 @@
         g.gkv[0, pl.ds(start, D)] += dot(grad_scores, queries) * SCALE
         g.gkv[1, pl.ds(start, D)] += dot(probs.astype(LOW), grad)
         grad_q = dot(grad_scores, keys, TN) * SCALE
-        at = pl.ds(pl.multiple_of(ROWS + start, 128), 128)
+        at = pl.ds(ROWS + start, 128)
         grad_q = turn_back(grad_q, twice(g.cos[at], 0), twice(g.sin[at], 0))
         back, slope = norm_back(g.qraw[b], g.heads[0:1], grad_q)
         g.dheads[0:1] += slope
         g.gqr[pl.ds(start, 128), 0:HD] = back[:128].astype(LOW)
         g.gqr[pl.ds(start, 128), HD : 2 * HD] = back[128:].astype(LOW)
-        return carry
 
     def back_block(b):
-        lax.fori_loop(b, b + 1, attend_back, 0)
+        attend_back(b)
         if b in (1, 3):
             rows = pl.ds(0, 256) if b == 1 else pl.ds(256, 768)
             g.kvs[rows] = g.gkv[1 - core, rows].astype(LOW)
@@ -773,6 +789,7 @@
         back, slope = norm_back(tok[rows].astype(F32), gain(0), total("n%d" % i, 1, rows))
         g.dgains[0:1] += slope
         igrad[rows] = g.gh[rows] + back
+        write(igrad.at[rows], igrad_hbm.at[rows])
 
     for i in range(2):
         jobs["V%d" % i] = lambda i=i: summed_rows(i)
@@ -828,6 +845,7 @@
             jobs[name + ".finish"]()
             cols = pl.ds(start, width)
             grads[:, at : at + width] = added(*(source[i, :, cols] for i in range(4)))
+            write(grads.at[:, pl.ds(at, width)], grads_hbm.at[:, pl.ds(at, width)])
 
         jobs[name + ".fin"] = work
 
@@ -844,6 +862,7 @@
         grads[:, 0:128] = jnp.where(core == 0, own, far)
         grads[:, EXTRA:OUT] = jnp.where(core == 0, far, own)
         grads[:, QUERY:EXTRA] = added(*(g.final[i, :, QUERY:EXTRA] for i in range(4)))
+        write(grads.at[:, pl.ds(0, OUT)], grads_hbm.at[:, pl.ds(0, OUT)])
 
     for name in ORDER:
         jobs[name]()
@@ -852,20 +871,47 @@
     for made in other.started:
         if not any(made is one for one in waited):
             made.wait_send()
-
-
-def hand_out(output, input_grad, done, ends, out, igrad, query, keyval, wide, gateup, down, norms, heads):
-    out[...] = output[...]
-    igrad[...] = input_grad[...]
+    for made in writes:
+        made.wait()
+
+
+def hand_out(output, input_grad, done_hbm, ends, *rest):
+    targets, norms, heads = rest[:7], rest[7], rest[8]
+    held, done, sems = rest[9:16], rest[16], rest[17]
+    out, igrad, query, keyval, wide, gateup, down = held
+    reads = [
+        pltpu.make_async_copy(a, b, sems.at[i])
+        for i, (a, b) in enumerate(((done_hbm, done), (input_grad, igrad), (output, out)))
+    ]
+    for made in reads:
+        made.start()
+    writes = [
+        pltpu.make_async_copy(a, b, sems.at[3 + i]) for i, (a, b) in enumerate(zip(held, targets))
+    ]
+    norms[...] = ends[0:4, 0:40]
+    heads[...] = ends[8:10, 0:16]
+    reads[0].wait()
+    gateup[0] = done[:40, GATEUP:DOWN]
+    gateup[1] = done[40:, GATEUP:DOWN]
+    writes[5].start()
+    down[...] = unfold(done[:, DOWN:WIRE])
+    writes[6].start()
     keyval[:, 0:256] = unfold(done[:, KV:QUERY])
     keyval[:, 256:512] = unfold(done[:, EXTRA:OUT])
     query[...] = unfold(done[:, QUERY:EXTRA])
     wide[...] = unfold(done[:, OUT:GATEUP])
-    gateup[0] = done[:40, GATEUP:DOWN]
-    gateup[1] = done[40:, GATEUP:DOWN]
-    down[...] = unfold(done[:, DOWN:WIRE])
-    norms[...] = ends[0:4, 0:40]
-    heads[...] = ends[8:10, 0:16]
+    for i in (2, 3, 4):
+        writes[i].start()
+    reads[1].wait()
+    writes[1].start()
+    reads[2].wait()
+    writes[0].start()
+    for made in writes:
+        made.wait()
+
+
+def anywhere():
+    return pl.BlockSpec(memory_space=pl.ANY)
 
 
 def vmem():
@@ -893,8 +939,8 @@
             jax.ShapeDtypeStruct((80, WIRE), F32),
             jax.ShapeDtypeStruct((16, 128), F32),
         ),
-        in_specs=[vmem()] * 10,
-        out_specs=(vmem(),) * 4,
+        in_specs=[anywhere(), vmem(), anywhere()] + [vmem()] * 7,
+        out_specs=(anywhere(),) * 3 + (vmem(),),
         scratch_shapes=[
             *(pltpu.VMEM(*shape) for shape in SCRATCH.values()),
             *ring_buffers(SET_COLS[0]),
@@ -905,6 +951,12 @@
             pltpu.SemaphoreType.DMA((128,)),
             pltpu.SemaphoreType.DMA((40,)),
             pltpu.SemaphoreType.DMA((40,)),
+            pltpu.VMEM((ROWS, D), LOW),
+            pltpu.VMEM((ROWS, D), LOW),
+            pltpu.VMEM((ROWS, D), LOW),
+            pltpu.VMEM((ROWS, D), F32),
+            pltpu.VMEM((80, WIRE), F32),
+            pltpu.SemaphoreType.DMA((16,)),
         ],
         compiler_params=pltpu.CompilerParams(
             collective_id=0, has_side_effects=True, vmem_limit_bytes=VMEM_BYTES
@@ -934,8 +986,19 @@
             jax.ShapeDtypeStruct((4, 40), F32),
             jax.ShapeDtypeStruct((2, 16), F32),
         ),
-        in_specs=[vmem()] * 4,
-        out_specs=(vmem(),) * 9,
+        in_specs=[anywhere()] * 3 + [vmem()],
+        out_specs=(anywhere(),) * 7 + (vmem(),) * 2,
+        scratch_shapes=[
+            pltpu.VMEM((ROWS, D), LOW),
+            pltpu.VMEM((ROWS, D), F32),
+            pltpu.VMEM((40, 512), F32),
+            pltpu.VMEM((40, 512), F32),
+            pltpu.VMEM((40, 512), F32),
+            pltpu.VMEM((2, 40, FFH), F32),
+            pltpu.VMEM((40, FFH), F32),
+            pltpu.VMEM((80, WIRE), F32),
+            pltpu.SemaphoreType.DMA((10,)),
+        ],
         compiler_params=pltpu.CompilerParams(vmem_limit_bytes=VMEM_BYTES),
     )(output, input_grad, done, ends)
     return (

time: 104 us -> 101 us (0.971)
  Pallas kernels: 103 us -> 99.7 us
    pallas_call x1, Pallas kernels: 99.9 us -> 95.5 us  [shards(): pl.pallas_call(layer_kernel, out_shape=(jax.ShapeDtypeStruct((ROWS, D), L...]
where the time goes in v4:
time: 101 us
  Pallas kernels  99.7 us (99%)
    pallas_call x1, Pallas kernels, shards(): pl.pallas_call(layer_kernel, out_shape=(jax.ShapeDtypeStruct((ROWS, D), L...  95.5 us
    pallas_call x1, Pallas kernels, shards(): pl.pallas_call(hand_out, out_shape=(jax.ShapeDtypeStruct((ROWS, D), LOW),...  4.19 us

profile of v4, /device:TPU:1, one launch (start us, length us, event | category | flops | bytes accessed | tf_op | source)
XLA Modules:
  0.0 100.5 jit_solution(250225525266145026)
XLA Ops:
  0.6 95.5 %shard_map.169 = (bf16[512,640]{1,0:T(8,128)(2,1)}, f32[512,640]{1,0:T(8,128)}, f32[80,2304]{1,0:T(8,128)}, f32[16,128]{1,0:T(8,128)}) custom-call(bf16[512,640]{1,0:T(8,128)(2,1)} %bitcast.8, s32[1,512]{1,0:T(1,128)} %seg_row.1, bf16[512,640]{1,0:T(8,128)(2,1)} %bitcast.9, bf16[40,512]{1,0:T(8,128)(2,1)} %wq.1, bf16[40,512]{1,0:T(8,128)(2,1)} %wkv.1, ...), custom_call_target="tpu_custom_call" | custom-call | tf_op jit(solution)/shard_map/pallas_call | solution.py:934
  96.1 4.2 %shard_map.170 = (bf16[512,640]{1,0:T(8,128)(2,1)}, f32[512,640]{1,0:T(8,128)}, f32[40,512]{1,0:T(8,128)}, f32[40,512]{1,0:T(8,128)}, f32[40,512]{1,0:T(8,128)},...) custom-call(bf16[512,640]{1,0:T(8,128)(2,1)} %get-tuple-element.22.output, ...), custom_call_target="tpu_custom_call" | custom-call | tf_op jit(solution)/shard_map/pallas_call | solution.py:976

commit v5 on v4

--- a/solution.py
+++ b/solution.py
@@ -13,19 +13,20 @@
 MESH = pl.DeviceIdType.MESH
 VMEM_BYTES = 60 * 1024 * 1024
 
-KV, QUERY, EXTRA, OUT, GATEUP, DOWN, WIRE = 0, 128, 384, 512, 768, 1792, 2304
+KV, QUERY, OUT, GATEUP, DOWN, WIRE = 0, 128, 384, 640, 1664, 2176
 GATHERS = (
-    ((0, 256), (256, 256)),
-    ((512, 128), (640, 128)),
-    ((768, 512), (1280, 512)),
-    ((1792, 256), (2048, 256)),
+    ((0, 128), (128, 128)),
+    ((256, 128), (384, 256)),
+    ((640, 512), (1152, 512)),
+    ((1664, 256), (1920, 256)),
 )
 SCATTERS = (
-    ("s3", (1792, 256), (2048, 256)),
-    ("sa", (768, 256), (1024, 256)),
-    ("sb", (1280, 256), (1536, 256)),
-    ("s1", (512, 128), (640, 128)),
-    ("s0", (0, 256), (256, 128)),
+    ("s3", (1664, 256), (1920, 256)),
+    ("sa", (640, 256), (896, 256)),
+    ("sb", (1152, 256), (1408, 256)),
+    ("s1", (384, 128), (512, 128)),
+    ("sq", (128, 128), (256, 128)),
+    ("sk", (0, 128), None),
 )
 SET_COLS = (1152, 1024)
 CUT = 48
@@ -283,7 +284,9 @@
 SCRATCH = dict(
     wire=((80, WIRE), LOW),
     whole=((4, 4, 80, WIRE), LOW),
-    tall=((128, 256), F32),
+    tile=((16, 128), F32),
+    tile_low=((16, 128), LOW),
+    tiles=((4, 4, 16, 128), LOW),
     wq=((D, 512), LOW),
     wkv=((D, HD), LOW),
     wo=((D, 512), LOW),
@@ -344,16 +347,16 @@
 
 
 ORDER = (
-    "w0", "w1", "p1.one", "p0.one", "w2", "p2.one", "tab", "mask", "p1.two", "w3", "p3.one",
-    "p0.three", "p2.two", "p1.three", "p3.two", "p0.four", "p2.three", "p1.four", "c0", "c1",
-    "p3.three", "c2", "A0", "A1", "p2.four", "c3", "A2", "A3", "c4", "h0", "p3.four", "h1",
-    "c6", "F0", "c8", "F1", "c9", "o0", "FB0", "G0", "o1", "P3", "s3.one", "FB1", "PA",
-    "sa.one", "PB", "sb.one", "G1", "N0", "s3.two", "B0", "sa.two", "B1", "sb.two", "N1", "B2",
-    "B3", "s3.three", "V0", "P1", "s1.one", "QS", "V1", "sa.three", "PQ", "KB", "s0.one",
-    "sb.three", "s3.four", "s1.two", "sa.four", "NN0", "s0.two", "sb.four", "s3.five", "NN1",
-    "I0", "s1.three", "sa.five", "I1", "EX", "se.one", "s0.three", "s3.fin", "s1.four",
-    "sb.five", "se.two", "s0.four", "sa.fin", "s1.five", "se.five", "s0.five", "sb.fin",
-    "s1.fin", "se.fin", "s0.fin",
+    "w0", "w1", "p1.one", "w2", "p0.one", "p2.one", "w3", "p3.one", "ge.one", "tab", "p1.three",
+    "p0.three", "ge.two", "p2.two", "p3.two", "p1.four", "p0.four", "p2.three", "p3.three",
+    "c0", "c1", "c2", "mask", "A0", "A1", "c3", "p2.four", "h0", "A2", "A3", "c4", "p3.four",
+    "h1", "c6", "F0", "c8", "F1", "c9", "o0", "FB0", "G0", "o1", "P3", "s3.one", "FB1", "PA",
+    "sa.one", "PB", "sb.one", "N0", "B0", "s3.two", "G1", "sa.two", "B1", "N1", "sb.two", "B2",
+    "B3", "s3.three", "P1", "s1.one", "QS", "V0", "V1", "sa.three", "PQ", "sq.one", "KB",
+    "sk.one", "sb.three", "s3.four", "s1.two", "sa.four", "sq.two", "NN0", "sb.four", "s3.five",
+    "NN1", "I0", "s1.three", "sk.two", "sa.five", "I1", "sq.three", "EX", "s1.four", "se.one",
+    "sb.five", "sk.three", "sq.four", "s3.fin", "s1.five", "se.two", "sa.fin", "sk.four",
+    "sq.five", "se.five", "sb.fin", "sk.five", "s1.fin", "sq.fin", "se.fin", "sk.fin",
 )
 
 
@@ -404,18 +407,19 @@
             jobs[name + "." + method] = lambda method=method: [getattr(m, method)() for m in members]
 
     for number, piece in enumerate(GATHERS):
-        steps(
-            "p%d" % number,
-            [
-                Gather(ring, gather_wires, g.wire, g.whole, number == 0, *piece[i])
-                for i, ring in enumerate(rings)
-            ],
-            ("one", "two", "three", "four", "finish"),
-        )
+        made = [
+            Gather(ring, gather_wires, g.wire, g.whole, number < 2, *piece[i])
+            for i, ring in enumerate(rings)
+        ]
+        steps("p%d" % number, made, ("one", "two", "three", "four", "finish"))
+        if number == 1:
+            p1 = made
     offsets = [0, 0]
     for name, *piece in SCATTERS:
         made = []
         for i, ring in enumerate(rings):
+            if piece[i] is None:
+                continue
             start, width = piece[i]
             far = (g.far.at[z], across) if start == KV else None
             made.append(
@@ -437,17 +441,30 @@
 
     @job("w0")
     def _():
-        g.tall[...] = jnp.zeros((128, 256), F32)
         mine = wkv[:, pl.ds(pl.multiple_of(core * HD, HD), HD)]
         g.wire[:, KV:QUERY] = fold(mine.astype(F32)).astype(LOW)
-        g.wire[:, QUERY:EXTRA] = fold(wq[...].astype(F32)).astype(LOW)
-        g.tall[0:4, 0:40] = ng[...].astype(F32)
-        g.tall[0:2, 128:144] = hg[...].astype(F32)
-        first = jnp.transpose(g.tall[:, 0:128])[:40]
-        second = jnp.transpose(g.tall[:, 128:256])[:40]
-        g.wire[:, EXTRA:OUT] = jnp.concatenate([first, second], axis=0).astype(LOW)
+        g.wire[:, QUERY:OUT] = fold(wq[...].astype(F32)).astype(LOW)
         g.whole[y, x, :, KV:OUT] = g.wire[:, KV:OUT]
+        g.tile[...] = jnp.zeros((16, 128), F32)
+        g.tile[0:4, 0:40] = ng[...].astype(F32)
+        g.tile[8:10, 0:16] = hg[...].astype(F32)
+        g.tile_low[...] = g.tile[...].astype(LOW)
         pl.semaphore_wait(barrier, len(targets))
+
+    @job("ge.one")
+    def _():
+        held["ge"] = [
+            other.copy(g.tile_low, g.tiles.at[y, x], {"dp": y * 4 + place(x + k)}) for k in (1, 3, 2)
+        ]
+
+    @job("ge.two")
+    def _():
+        for made in held["ge"]:
+            made.wait_recv()
+        g.tiles[y, x] = g.tile_low[...]
+        held["ge"] = [
+            other.copy(g.tiles.at[y], g.tiles.at[y], {"dp": place(y + k) * 4 + x}) for k in (1, 3, 2)
+        ]
 
     @job("w1")
     def _():
@@ -526,12 +543,12 @@
     @job("c0")
     def _():
         jobs["p0.finish"]()
-        block = g.whole[:, :, :, EXTRA:OUT].astype(F32)
-        g.gains[...] = jnp.transpose(block[:, :, :40].reshape(D, 128))[:8]
-        spread = jnp.transpose(block[:, :, 40:].reshape(D, 128))[:8]
-        column_at, head_at = iota((D, HD), 0), iota((D, HD), 1)
-        pick = (column_at == 40 * (head_at >> 4) + (head_at & 15)).astype(F32).astype(LOW)
-        g.heads[...] = dot(spread.astype(LOW), pick)
+        for made in held["ge"]:
+            made.wait_recv()
+        for d in range(16):
+            block = g.tiles[d // 4, d % 4].astype(F32)
+            g.gains[:, 40 * d : 40 * d + 40] = block[0:8, 0:40]
+            g.heads[:, 16 * d : 16 * d + 16] = block[8:16, 0:16]
         assemble(g.wkv, None, KV, 128)
         for rows in halves:
             block = tok[rows].astype(F32)
@@ -550,6 +567,7 @@
 
     @job("c2")
     def _():
+        p1[0].finish()
         assemble(g.wq, None, QUERY, 256)
         for i in range(2):
             at = slice(ROWS + 256 * i, ROWS + 256 * i + 256)
@@ -589,7 +607,7 @@
 
     @job("c3")
     def _():
-        jobs["p1.finish"]()
+        p1[1].finish()
         assemble(g.wo, None, OUT, 256)
         swap("a0", 0, halves[0], dot(g.o[halves[0]], g.wo[...], NT))
 
@@ -854,15 +872,17 @@
     put_final("sb", g.final, GATEUP + 512, GATEUP + 512, 512)
     put_final("s1", g.final, OUT, OUT, 256)
 
-    @job("s0.fin")
-    def _():
-        jobs["s0.finish"]()
+    put_final("sq", g.final, QUERY, QUERY, 256)
+
+    @job("sk.fin")
+    def _():
+        jobs["sk.finish"]()
         own = added(*(g.final[i, :, KV:QUERY] for i in range(4)))
         far = added(*(g.far[i] for i in range(4)))
         grads[:, 0:128] = jnp.where(core == 0, own, far)
-        grads[:, EXTRA:OUT] = jnp.where(core == 0, far, own)
-        grads[:, QUERY:EXTRA] = added(*(g.final[i, :, QUERY:EXTRA] for i in range(4)))
-        write(grads.at[:, pl.ds(0, OUT)], grads_hbm.at[:, pl.ds(0, OUT)])
+        grads[:, WIRE : WIRE + 128] = jnp.where(core == 0, far, own)
+        for cols in (pl.ds(0, 128), pl.ds(WIRE, 128)):
+            write(grads.at[:, cols], grads_hbm.at[:, cols])
 
     for name in ORDER:
         jobs[name]()
@@ -875,39 +895,18 @@
         made.wait()
 
 
-def hand_out(output, input_grad, done_hbm, ends, *rest):
-    targets, norms, heads = rest[:7], rest[7], rest[8]
-    held, done, sems = rest[9:16], rest[16], rest[17]
-    out, igrad, query, keyval, wide, gateup, down = held
-    reads = [
-        pltpu.make_async_copy(a, b, sems.at[i])
-        for i, (a, b) in enumerate(((done_hbm, done), (input_grad, igrad), (output, out)))
-    ]
-    for made in reads:
-        made.start()
-    writes = [
-        pltpu.make_async_copy(a, b, sems.at[3 + i]) for i, (a, b) in enumerate(zip(held, targets))
-    ]
+def hand_out(output, input_grad, done, ends, out, igrad, query, keyval, wide, gateup, down, norms, heads):
+    out[...] = output[...]
+    igrad[...] = input_grad[...]
+    keyval[:, 0:256] = unfold(done[:, KV:QUERY])
+    keyval[:, 256:512] = unfold(done[:, WIRE : WIRE + 128])
+    query[...] = unfold(done[:, QUERY:OUT])
+    wide[...] = unfold(done[:, OUT:GATEUP])
+    gateup[0] = done[:40, GATEUP:DOWN]
+    gateup[1] = done[40:, GATEUP:DOWN]
+    down[...] = unfold(done[:, DOWN:WIRE])
     norms[...] = ends[0:4, 0:40]
     heads[...] = ends[8:10, 0:16]
-    reads[0].wait()
-    gateup[0] = done[:40, GATEUP:DOWN]
-    gateup[1] = done[40:, GATEUP:DOWN]
-    writes[5].start()
-    down[...] = unfold(done[:, DOWN:WIRE])
-    writes[6].start()
-    keyval[:, 0:256] = unfold(done[:, KV:QUERY])
-    keyval[:, 256:512] = unfold(done[:, EXTRA:OUT])
-    query[...] = unfold(done[:, QUERY:EXTRA])
-    wide[...] = unfold(done[:, OUT:GATEUP])
-    for i in (2, 3, 4):
-        writes[i].start()
-    reads[1].wait()
-    writes[1].start()
-    reads[2].wait()
-    writes[0].start()
-    for made in writes:
-        made.wait()
 
 
 def anywhere():
@@ -936,7 +935,7 @@
         out_shape=(
             jax.ShapeDtypeStruct((ROWS, D), LOW),
             jax.ShapeDtypeStruct((ROWS, D), F32),
-            jax.ShapeDtypeStruct((80, WIRE), F32),
+            jax.ShapeDtypeStruct((80, WIRE + 128), F32),
             jax.ShapeDtypeStruct((16, 128), F32),
         ),
         in_specs=[anywhere(), vmem(), anywhere()] + [vmem()] * 7,
@@ -955,7 +954,7 @@
             pltpu.VMEM((ROWS, D), LOW),
             pltpu.VMEM((ROWS, D), LOW),
             pltpu.VMEM((ROWS, D), F32),
-            pltpu.VMEM((80, WIRE), F32),
+            pltpu.VMEM((80, WIRE + 128), F32),
             pltpu.SemaphoreType.DMA((16,)),
         ],
         compiler_params=pltpu.CompilerParams(
@@ -986,19 +985,8 @@
             jax.ShapeDtypeStruct((4, 40), F32),
             jax.ShapeDtypeStruct((2, 16), F32),
         ),
-        in_specs=[anywhere()] * 3 + [vmem()],
-        out_specs=(anywhere(),) * 7 + (vmem(),) * 2,
-        scratch_shapes=[
-            pltpu.VMEM((ROWS, D), LOW),
-            pltpu.VMEM((ROWS, D), F32),
-            pltpu.VMEM((40, 512), F32),
-            pltpu.VMEM((40, 512), F32),
-            pltpu.VMEM((40, 512), F32),
-            pltpu.VMEM((2, 40, FFH), F32),
-            pltpu.VMEM((40, FFH), F32),
-            pltpu.VMEM((80, WIRE), F32),
-            pltpu.SemaphoreType.DMA((10,)),
-        ],
+        in_specs=[vmem()] * 4,
+        out_specs=(vmem(),) * 9,
         compiler_params=pltpu.CompilerParams(vmem_limit_bytes=VMEM_BYTES),
     )(output, input_grad, done, ends)
     return (

time: 101 us -> 98.3 us (0.973)
  Pallas kernels: 99.7 us -> 97.5 us
    pallas_call x1, Pallas kernels: 95.5 us -> 94.2 us  [shards(): pl.pallas_call(layer_kernel, out_shape=(jax.ShapeDtypeStruct((ROWS, D), L...]
where the time goes in v5:
time: 98.3 us; the launch traced here: 98.2 us
  Pallas kernels  97.5 us (99%)
    pallas_call x1, Pallas kernels, shards(): pl.pallas_call(layer_kernel, out_shape=(jax.ShapeDtypeStruct((ROWS, D), L...  94.2 us
    pallas_call x1, Pallas kernels, shards(): pl.pallas_call(hand_out, out_shape=(jax.ShapeDtypeStruct((ROWS, D), LOW),...  3.31 us

profile of v5, /device:TPU:1, one launch (start us, length us, event | category | flops | bytes accessed | tf_op | source)
XLA Modules:
  0.0 98.2 jit_solution(8904089812617681174)
XLA Ops:
  0.6 94.2 %shard_map.169 = (bf16[512,640]{1,0:T(8,128)(2,1)}, f32[512,640]{1,0:T(8,128)}, f32[80,2304]{1,0:T(8,128)}, f32[16,128]{1,0:T(8,128)}) custom-call(bf16[512,640]{1,0:T(8,128)(2,1)} %bitcast.8, s32[1,512]{1,0:T(1,128)} %seg_row.1, bf16[512,640]{1,0:T(8,128)(2,1)} %bitcast.9, bf16[40,512]{1,0:T(8,128)(2,1)} %wq.1, bf16[40,512]{1,0:T(8,128)(2,1)} %wkv.1, ...), custom_call_target="tpu_custom_call" | custom-call | tf_op jit(solution)/shard_map/pallas_call | solution.py:933
  94.8 3.3 %shard_map.170 = (bf16[512,640]{1,0:T(8,128)(2,1)}, f32[512,640]{1,0:T(8,128)}, f32[40,512]{1,0:T(8,128)}, f32[40,512]{1,0:T(8,128)}, f32[40,512]{1,0:T(8,128)},...) custom-call(bf16[512,640]{1,0:T(8,128)(2,1)} %get-tuple-element.22.output, ...), custom_call_target="tpu_custom_call" | custom-call | tf_op jit(solution)/shard_map/pallas_call | solution.py:975

commit v6 on v5

--- a/solution.py
+++ b/solution.py
@@ -347,16 +347,16 @@
 
 
 ORDER = (
-    "w0", "w1", "p1.one", "w2", "p0.one", "p2.one", "w3", "p3.one", "ge.one", "tab", "p1.three",
-    "p0.three", "ge.two", "p2.two", "p3.two", "p1.four", "p0.four", "p2.three", "p3.three",
-    "c0", "c1", "c2", "mask", "A0", "A1", "c3", "p2.four", "h0", "A2", "A3", "c4", "p3.four",
+    "w0", "p0.one", "w1", "w2", "p2.one", "tab", "p1.one", "mask", "p0.three", "w3", "ge.one",
+    "p3.one", "p2.two", "p1.three", "ge.two", "p0.four", "p3.two", "p2.three", "p1.four", "c0",
+    "p3.three", "c1", "p2.four", "c2", "A0", "A1", "A2", "c3", "A3", "c4", "p3.four", "h0",
     "h1", "c6", "F0", "c8", "F1", "c9", "o0", "FB0", "G0", "o1", "P3", "s3.one", "FB1", "PA",
-    "sa.one", "PB", "sb.one", "N0", "B0", "s3.two", "G1", "sa.two", "B1", "N1", "sb.two", "B2",
-    "B3", "s3.three", "P1", "s1.one", "QS", "V0", "V1", "sa.three", "PQ", "sq.one", "KB",
-    "sk.one", "sb.three", "s3.four", "s1.two", "sa.four", "sq.two", "NN0", "sb.four", "s3.five",
-    "NN1", "I0", "s1.three", "sk.two", "sa.five", "I1", "sq.three", "EX", "s1.four", "se.one",
-    "sb.five", "sk.three", "sq.four", "s3.fin", "s1.five", "se.two", "sa.fin", "sk.four",
-    "sq.five", "se.five", "sb.fin", "sk.five", "s1.fin", "sq.fin", "se.fin", "sk.fin",
+    "sa.one", "N0", "PB", "sb.one", "G1", "s3.two", "B0", "sa.two", "B1", "sb.two", "N1", "B2",
+    "B3", "s3.three", "PQ", "sq.one", "V0", "P1", "s1.one", "sa.three", "V1", "QS", "KB",
+    "sk.one", "sb.three", "s3.four", "sq.two", "s1.two", "sa.four", "sb.four", "NN0", "s3.five",
+    "NN1", "sq.three", "I0", "sk.two", "s1.three", "sa.five", "I1", "sq.four", "EX", "se.one",
+    "sb.five", "sk.three", "s1.four", "s3.fin", "sq.five", "se.two", "sa.fin", "sk.four",
+    "s1.five", "se.five", "sb.fin", "sk.five", "sq.fin", "s1.fin", "se.fin", "sk.fin",
 )
 
 

time: 98.3 us -> 99.6 us (1.013)
  Pallas kernels: 97.5 us -> 98.8 us
    pallas_call x1, Pallas kernels: 94.2 us -> 95.5 us  [shards(): pl.pallas_call(layer_kernel, out_shape=(jax.ShapeDtypeStruct((ROWS, D), L...]
where the time goes in v6:
time: 99.6 us; the launch traced here: 99.5 us
  Pallas kernels  98.8 us (99%)
    pallas_call x1, Pallas kernels, shards(): pl.pallas_call(layer_kernel, out_shape=(jax.ShapeDtypeStruct((ROWS, D), L...  95.5 us
    pallas_call x1, Pallas kernels, shards(): pl.pallas_call(hand_out, out_shape=(jax.ShapeDtypeStruct((ROWS, D), LOW),...  3.31 us

profile of v6, /device:TPU:1, one launch (start us, length us, event | category | flops | bytes accessed | tf_op | source)
XLA Modules:
  0.0 99.5 jit_solution(10337642159418942807)
XLA Ops:
  0.6 95.5 %shard_map.169 = (bf16[512,640]{1,0:T(8,128)(2,1)}, f32[512,640]{1,0:T(8,128)}, f32[80,2304]{1,0:T(8,128)}, f32[16,128]{1,0:T(8,128)}) custom-call(bf16[512,640]{1,0:T(8,128)(2,1)} %bitcast.8, s32[1,512]{1,0:T(1,128)} %seg_row.1, bf16[512,640]{1,0:T(8,128)(2,1)} %bitcast.9, bf16[40,512]{1,0:T(8,128)(2,1)} %wq.1, bf16[40,512]{1,0:T(8,128)(2,1)} %wkv.1, ...), custom_call_target="tpu_custom_call" | custom-call | tf_op jit(solution)/shard_map/pallas_call | solution.py:933
  96.1 3.3 %shard_map.170 = (bf16[512,640]{1,0:T(8,128)(2,1)}, f32[512,640]{1,0:T(8,128)}, f32[40,512]{1,0:T(8,128)}, f32[40,512]{1,0:T(8,128)}, f32[40,512]{1,0:T(8,128)},...) custom-call(bf16[512,640]{1,0:T(8,128)(2,1)} %get-tuple-element.22.output, ...), custom_call_target="tpu_custom_call" | custom-call | tf_op jit(solution)/shard_map/pallas_call | solution.py:975
